TPU v7x, 512 devices: a whole 4x4x16 slice. The times are simulated.
512 devices in a mesh: leaf: 128 (over y, z, core), blk: 4 (over x).
Axes of the slice: x: 4, y: 4, z: 16, core: 2. Of those that a mesh axis runs over, the one named last changes fastest.
Arguments:
- leaf_basis: bfloat16 [2048, 64, 512], P('leaf'), may hold values from -13 to 13
- leaf_pairing: int32 [128, 16], P('leaf'), may hold values from 0 to 15, each once within a row
- leaf_transfer: float32 [2048, 64, 64], P('leaf'), may hold values from -2 to 2
- inner_transfer: float32 [128, 15, 64, 64], P('leaf'), may hold values from -2 to 2
- upper_transfer: bfloat16 [128, 64, 64], replicated, may hold values from -2 to 2
- coupling: bfloat16 [2048, 16, 64, 64], P('leaf', 'blk'), may hold values from -0.29882812 to 0.29882812
- source_cluster_index: int32 [2048, 16], P('leaf', 'blk'), may hold values from 0 to 2047, as said below
- coupling_slot_mask: int32 [2048, 16], P('leaf', 'blk'), may hold values 0 or 1
Outputs:
- scaled_orthogonal_basis: bfloat16 [2048, 64, 512], P('leaf', None, 'blk')
- inner_cluster_factor: float32 [128, 15, 64, 64], P('leaf')
- parent_upper_factor: float32 [128, 7, 64, 64], P('leaf')
- projected: bfloat16 [2048, 16, 64, 64], P('leaf', 'blk')
- target_row_weight: float32 [2048, 64, 64], P(('leaf', 'blk'))
Inputs may be any that keep to these rules, and one draw needn't show every extreme that they name: Each row of leaf_pairing is a permutation of 0 to 15. source_cluster_index[t, s] differs from t by 1 to 8, and by exactly 8 in slot 0.
All inputs are finite; a program needn't handle non-finite values. No bound on the sum of `coupling_slot_mask` on one device may be relied on, other than what follows from the above.
Results may differ from a plain program's by a relative error of at most 0.013.
Values may be sent and summed in bfloat16 or wider, within the bound.
A program may use at most 64 MiB of HBM per device.

v0:
```python
import math

import jax
import jax.numpy as jnp
from jax import lax
from jax.sharding import PartitionSpec as P

highest_precision = lax.Precision.HIGHEST


def swapped(shard, axis, apart):
    return lax.ppermute(shard, axis, [(i, i ^ 1 << apart) for i in range(lax.axis_size(axis))])


def extended_2(cells, sides, width):
    for axis, dim in sides:
        count = lax.axis_size(axis)
        ends = count - 1
        head = lax.slice_in_dim(cells, 0, width, axis=dim)
        tail = lax.slice_in_dim(cells, cells.shape[dim] - width, cells.shape[dim], axis=dim)
        cells = jnp.concatenate(
            [
                lax.ppermute(tail, axis, [(i, (i + 1) % count) for i in range(ends)]),
                cells,
                lax.ppermute(head, axis, [((i + 1) % count, i) for i in range(ends)]),
            ],
            axis=dim,
        )
    return cells


def carry_up(transfer, gram_in):
    left_part = jnp.einsum("nba,nbc->nac", transfer, gram_in, precision=highest_precision)
    return jnp.einsum("nac,ncd->nad", left_part, transfer, precision=highest_precision)


def pair_sum(term_stack):
    node_count = term_stack.shape[0] // 2
    paired = term_stack.reshape(node_count, 2, term_stack.shape[1], term_stack.shape[2])
    return paired[:, 0] + paired[:, 1]


def triangle_of(gram_in):
    order_size = gram_in.shape[-1]
    positions = jnp.arange(order_size, dtype=jnp.int32)

    def column_step(column, state):
        working, lower_part = state
        marker = (positions == column).astype(jnp.float32)
        column_vals = jnp.sum(working * marker, axis=-1)
        pivot_value = jnp.sum(column_vals * marker, axis=-1)
        scaled_column = jnp.where(
            positions >= column, column_vals / jnp.sqrt(pivot_value)[..., None], 0.0
        )
        lower_part = lower_part + scaled_column[..., :, None] * marker
        working = working - scaled_column[..., :, None] * scaled_column[..., None, :]
        return (working, lower_part)

    start_lower = jnp.zeros(gram_in.shape, jnp.float32)
    final_state = lax.fori_loop(0, order_size, column_step, (gram_in, start_lower))
    return jnp.swapaxes(final_state[1], -1, -2)


def inverse_of(factor):
    order_size = factor.shape[-1]
    positions = jnp.arange(order_size, dtype=jnp.int32)
    lower_part = jnp.swapaxes(factor, -1, -2)

    def row_step(row_index, solved):
        marker = (positions == row_index).astype(jnp.float32)
        row_vals = jnp.sum(lower_part * marker[:, None], axis=-2)
        pivot_value = jnp.sum(row_vals * marker, axis=-1)
        earlier = jnp.where(positions < row_index, row_vals, 0.0)
        partial_row = jnp.einsum("...j,...jc->...c", earlier, solved, precision=highest_precision)
        new_row = (marker - partial_row) / pivot_value[..., None]
        return solved + marker[:, None] * new_row[..., None, :]

    solved_lower = lax.fori_loop(0, order_size, row_step, jnp.zeros(factor.shape, jnp.float32))
    return jnp.swapaxes(solved_lower, -1, -2)


def select_rows(order, table):
    choose = (order[:, None] == jnp.arange(table.shape[0], dtype=jnp.int32)[None, :]).astype(
        jnp.float32
    )
    return jnp.einsum("ml,lab->mab", choose, table, precision=highest_precision)


def local_tree(gram_leaf, leaf_order, leaf_moves, inner_moves):
    ordered_gram = select_rows(leaf_order, gram_leaf)
    ordered_move = select_rows(leaf_order, leaf_moves)
    level_gram = pair_sum(carry_up(ordered_move, ordered_gram))
    level_list = [level_gram]
    slot_offset = 0
    while level_gram.shape[0] > 1:
        node_count = level_gram.shape[0]
        level_gram = pair_sum(
            carry_up(inner_moves[slot_offset : slot_offset + node_count], level_gram)
        )
        slot_offset = slot_offset + node_count
        level_list.append(level_gram)
    node_grams = jnp.concatenate(level_list, axis=0)
    root_term = carry_up(inner_moves[slot_offset : slot_offset + 1], level_gram)[0]
    return (node_grams, root_term)


def local(
    leaf_basis,
    leaf_pairing,
    leaf_transfer,
    inner_transfer,
    upper_transfer,
    coupling,
    source_cluster_index,
    coupling_slot_mask,
):
    leaves = leaf_basis.shape[0]
    panels = leaf_basis.shape[2]
    blocks = lax.axis_size("blk")
    panel_part = panels // blocks
    block_index = lax.axis_index("blk")
    panel_slice = lax.dynamic_slice_in_dim(leaf_basis, block_index * panel_part, panel_part, 2)
    gram_leaf = jnp.einsum(
        "lkp,ljp->lkj", leaf_basis, leaf_basis, preferred_element_type=jnp.float32
    )
    node_grams, root_term = local_tree(gram_leaf, leaf_pairing[0], leaf_transfer, inner_transfer[0])
    all_factors = triangle_of(jnp.concatenate([gram_leaf, node_grams], axis=0))
    leaf_factor = all_factors[:leaves]
    inner_cluster_factor = all_factors[leaves:][None]
    weights = (math.sqrt(panels) * inverse_of(leaf_factor)).astype(jnp.bfloat16)
    scaled_orthogonal_basis = jnp.einsum(
        "lkj,lkp->ljp", weights, panel_slice, preferred_element_type=jnp.float32
    ).astype(jnp.bfloat16)
    leaf_count = lax.axis_size("leaf")
    tree_depth = leaf_count.bit_length() - 1
    device_index = lax.axis_index("leaf")
    level_grams = []
    owned_gram = root_term
    for tree_level in range(1, tree_depth + 1):
        if tree_level > 1:
            stride = 2 ** (tree_level - 1)
            owner_row = device_index // stride * stride + stride // 2
            own_move = lax.dynamic_index_in_dim(
                upper_transfer, owner_row, 0, keepdims=False
            ).astype(jnp.float32)
            owned_gram = carry_up(own_move[None], owned_gram[None])[0]
        partner_gram = swapped(owned_gram, "leaf", tree_level - 1)
        owned_gram = owned_gram + partner_gram
        level_grams.append(owned_gram)
    parent_upper_factor = triangle_of(jnp.stack(level_grams, axis=0))[None]
    lower_factor_half = leaf_factor.astype(jnp.bfloat16)
    halo_width = leaves // 2
    extended = extended_2(lower_factor_half, (("leaf", 0),), halo_width)
    local_index = source_cluster_index - (device_index * leaves - halo_width)
    choose_source = (
        local_index[:, :, None] == jnp.arange(extended.shape[0], dtype=jnp.int32)[None, None, :]
    ).astype(jnp.bfloat16)
    source_low = jnp.einsum(
        "tse,eab->tsab", choose_source, extended, preferred_element_type=jnp.float32
    ).astype(jnp.bfloat16)
    half_proj = jnp.einsum(
        "tab,tsbc->tsac", lower_factor_half, coupling, preferred_element_type=jnp.float32
    ).astype(jnp.bfloat16)
    full_proj = jnp.einsum(
        "tsac,tsdc->tsad", half_proj, source_low, preferred_element_type=jnp.float32
    )
    projected = (full_proj * coupling_slot_mask.astype(jnp.float32)[:, :, None, None]).astype(
        jnp.bfloat16
    )
    slots_here = source_cluster_index.shape[1]
    row_scale = 1.0 / (slots_here * blocks * leaf_basis.shape[1])
    target_row_weight = lax.psum_scatter(
        (
            jnp.einsum("lfdv,lfrv->ldr", projected, projected, preferred_element_type=jnp.float32)
            * row_scale
        ).astype(jnp.bfloat16),
        "blk",
        scatter_dimension=0,
        tiled=True,
    ).astype(jnp.float32)
    return (
        scaled_orthogonal_basis,
        inner_cluster_factor,
        parent_upper_factor,
        projected,
        target_row_weight,
    )


def solution(mesh):
    placed = (
        P("leaf", None, None),
        P("leaf", None),
        P("leaf", None, None),
        P("leaf", None, None, None),
        P(),
        P("leaf", "blk", None, None),
        P("leaf", "blk"),
        P("leaf", "blk"),
    )
    return jax.shard_map(
        local,
        mesh=mesh,
        in_specs=placed,
        out_specs=(
            P("leaf", None, "blk"),
            P("leaf", None, None, None),
            P("leaf", None, None, None),
            P("leaf", "blk", None, None),
            P(("leaf", "blk"), None, None),
        ),
        check_vma=False,
    )
```

profile of v0, /device:TPU:6, one launch (start us, length us, event | category | flops | bytes accessed | tf_op | source)
XLA Modules:
  0.0 293.2 jit_solution(6585373893604987159)
XLA Ops:
  10.5 1.3 fusion.16
  16.1 1.9 collective-permute-start
  19.1 80.2 %while.49 = (s32[]{:T(128)}, f32[31,64,64]{2,1,0:T(8,128)S(1)}, f32[31,64,64]{2,1,0:T(8,128)S(1)}, s32[]{:T(128)}, s32[]{:T(128)}) while((s32[]{:T(128)}, f32[31,64,64]{2,1,0:T(8,128)S(1)}, f32[31,64,64]{2,1,0:T(8,128)S(1)}, s32[]{:T(128)}, s32[]{:T(128)}) %tuple.126), condition=%wide.region_3.4_spmd.clone.clone, body=%wide.region_0.3_spmd.clone.clone.sunk | while | flops 894948 | bytes 2580923 | solution.py:60
  101.2 3.0 %collective-permute-start.7 = (bf16[8,64,64]{2,1,0:T(8,128)(2,1)}, bf16[8,64,64]{2,1,0:T(8,128)(2,1)}, u32[]{:S(2)}, u32[]{:S(2)}) collective-permute-start(bf16[8,64,64]{2,1,0:T(8,128)(2,1)} %get-tuple-element.374), channel_id=1, source_target_pairs={{0,4},{4,8},{8,12},{12,16},{16,20},{20,24},{24,28},{28,32},{32,36}... | collective-permute-start | bytes 196616 | tf_op jit(solution)/shard_map/ppermute | solution.py:23
  104.3 1.5 collective-permute-start.8
  105.8 1.9 slice_bitcast_fusion.1
  108.0 66.3 %while.50 = (s32[]{:T(128)}, f32[16,64,64]{2,1,0:T(8,128)S(1)}, f32[16,64,64]{2,1,0:T(8,128)S(1)}, s32[]{:T(128)}, s32[]{:T(128)}) while((s32[]{:T(128)}, f32[16,64,64]{2,1,0:T(8,128)S(1)}, f32[16,64,64]{2,1,0:T(8,128)S(1)}, s32[]{:T(128)}, s32[]{:T(128)}) %tuple.129), condition=%wide.region_7.8_spmd.clone.clone, body=%wide.region_4.7_spmd.clone.clone.sunk | while | flops 1183923 | bytes 1082956 | solution.py:78
  175.5 4.7 %constant_dynamic-slice_fusion = (bf16[1,64,64]{0,2,1:T(8,128)(2,1)}, bf16[1,64,64]{0,2,1:T(8,128)(2,1)}, bf16[1,64,64]{0,2,1:T(8,128)(2,1)}, bf16[1,64,64]{0,2,...) fusion(bf16[128,64,64]{0,2,1:T(8,128)(2,1)S(1)} %copy-done.1, s32[]{:T(128)S(6)} %select_n.98, ...), kind=kLoop, calls=%fused_computation.143 | loop fusion | bytes 98328 | tf_op jit(solution)/shard_map/jit(dynamic_index_in_dim)/dynamic_slice | solution.py:143
  180.3 1.8 copy.55
  183.1 1.8 copy.58
  187.0 5.1 %collective-permute-start.1 = (f32[64,64]{1,0:T(8,128)S(1)}, f32[64,64]{1,0:T(8,128)S(1)}, u32[]{:S(2)}, u32[]{:S(2)}) collective-permute-start(f32[64,64]{1,0:T(8,128)S(1)} %fusion.86), channel_id=1, source_target_pairs={{0,8},{4,12},{8,0},{12,4},{16,24},{20,28},{24,16},{28,20},{32,40},... | collective-permute-start | bytes 49160 | tf_op jit(solution)/shard_map/ppermute | solution.py:12
  194.4 5.3 %collective-permute-start.2 = (f32[64,64]{1,0:T(8,128)S(1)}, f32[64,64]{1,0:T(8,128)S(1)}, u32[]{:S(2)}, u32[]{:S(2)}) collective-permute-start(f32[64,64]{1,0:T(8,128)S(1)} %fusion.82), channel_id=1, source_target_pairs={{0,16},{4,20},{8,24},{12,28},{16,0},{20,4},{24,8},{28,12},{32,48},... | collective-permute-start | bytes 49160 | tf_op jit(solution)/shard_map/ppermute | solution.py:12
  199.7 2.0 collective-permute-done.2
  202.1 10.4 %collective-permute-start.3 = (f32[64,64]{1,0:T(8,128)S(1)}, f32[64,64]{1,0:T(8,128)S(1)}, u32[]{:S(2)}, u32[]{:S(2)}) collective-permute-start(f32[64,64]{1,0:T(8,128)S(1)} %fusion.78), channel_id=1, source_target_pairs={{0,32},{4,36},{8,40},{12,44},{16,48},{20,52},{24,56},{28,60},{32,0... | collective-permute-start | bytes 49160 | tf_op jit(solution)/shard_map/ppermute | solution.py:12
  212.5 2.1 collective-permute-done.3
  215.0 14.0 %collective-permute-start.4 = (f32[64,64]{1,0:T(8,128)S(1)}, f32[64,64]{1,0:T(8,128)S(1)}, u32[]{:S(2)}, u32[]{:S(2)}) collective-permute-start(f32[64,64]{1,0:T(8,128)S(1)} %fusion.74), channel_id=1, source_target_pairs={{0,64},{4,68},{8,72},{12,76},{16,80},{20,84},{24,88},{28,92},{32,9... | collective-permute-start | bytes 49160 | tf_op jit(solution)/shard_map/ppermute | solution.py:12
  230.1 1.5 fusion.14
  231.6 2.7 multiply_convert_fusion
  235.8 3.5 %collective-permute-start.5 = (f32[64,64]{1,0:T(8,128)S(1)}, f32[64,64]{1,0:T(8,128)S(1)}, u32[]{:S(2)}, u32[]{:S(2)}) collective-permute-start(f32[64,64]{1,0:T(8,128)S(1)} %fusion.70), channel_id=1, source_target_pairs={{0,128},{4,132},{8,136},{12,140},{16,144},{20,148},{24,152},{28,15... | collective-permute-start | bytes 49160 | tf_op jit(solution)/shard_map/ppermute | solution.py:12
  239.3 2.5 collective-permute-done.5
  242.2 4.9 %collective-permute-start.6 = (f32[64,64]{1,0:T(8,128)S(1)}, f32[64,64]{1,0:T(8,128)S(1)}, u32[]{:S(2)}, u32[]{:S(2)}) collective-permute-start(f32[64,64]{1,0:T(8,128)S(1)} %fusion.66), channel_id=1, source_target_pairs={{0,256},{4,260},{8,264},{12,268},{16,272},{20,276},{24,280},{28,28... | collective-permute-start | bytes 49160 | tf_op jit(solution)/shard_map/ppermute | solution.py:12
  247.1 2.4 collective-permute-done.6
  249.5 34.4 %while.51 = (s32[]{:T(128)}, f32[7,64,64]{2,1,0:T(8,128)S(1)}, f32[7,64,64]{2,1,0:T(8,128)S(1)}, s32[]{:T(128)}, s32[]{:T(128)}) while((s32[]{:T(128)}, f32[7,64,64]{2,1,0:T(8,128)S(1)}, f32[7,64,64]{2,1,0:T(8,128)S(1)}, s32[]{:T(128)}, s32[]{:T(128)}) %tuple.132), condition=%wide.region_11.12_spmd.clone.clone, body=%wide.region_8.11_spmd.clone.clone.sunk | while | flops 202236 | bytes 583739 | solution.py:60
  284.8 1.5 convert_element_type.100
  (1248 shorter events, 195.7 us)
Async XLA Ops:
  7.2 1.2 copy-start
  7.2 1.7 copy-start.13
  7.2 277.6 %reduce-scatter.2.cloned.1.call-start = ((), (), s32[]{:S(2)}) async-start(), calls=%async_computation.1 | async-start | bytes 327680 | tf_op jit(solution)/shard_map/reduce_scatter | solution.py:172
  8.8 1.0 copy-start.12
  11.8 1.0 copy-start.11
  12.6 1.9 copy-start.8
  16.1 169.8 %collective-permute-start = (f32[64,64]{1,0:T(8,128)}, f32[64,64]{1,0:T(8,128)}, u32[]{:S(2)}, u32[]{:S(2)}) collective-permute-start(f32[64,64]{1,0:T(8,128)} %fusion.56), channel_id=1, source_target_pairs={{0,4},{4,0},{8,12},{12,8},{16,20},{20,16},{24,28},{28,24},{32,36},... | collective-permute-start | bytes 49160 | tf_op jit(solution)/shard_map/ppermute | solution.py:12
  99.7 6.1 %copy-start.3 = (f32[31,64,64]{1,2,0:T(8,128)}, f32[31,64,64]{1,2,0:T(8,128)S(1)}, u32[]{:S(2)}) copy-start(f32[31,64,64]{1,2,0:T(8,128)S(1)} %copy.28) | copy-start | bytes 1523716
  101.2 127.8 %collective-permute-start.7 = (bf16[8,64,64]{2,1,0:T(8,128)(2,1)}, bf16[8,64,64]{2,1,0:T(8,128)(2,1)}, u32[]{:S(2)}, u32[]{:S(2)}) collective-permute-start(bf16[8,64,64]{2,1,0:T(8,128)(2,1)} %get-tuple-element.374), channel_id=1, source_target_pairs={{0,4},{4,8},{8,12},{12,16},{16,20},{20,24},{24,28},{28,32},{32,36}... | collective-permute-start | bytes 196616 | tf_op jit(solution)/shard_map/ppermute | solution.py:23
  104.3 124.7 %collective-permute-start.8 = (bf16[8,64,64]{2,1,0:T(8,128)(2,1)}, bf16[8,64,64]{2,1,0:T(8,128)(2,1)}, u32[]{:S(2)}, u32[]{:S(2)}) collective-permute-start(bf16[8,64,64]{2,1,0:T(8,128)(2,1)} %get-tuple-element.375), channel_id=1, source_target_pairs={{4,0},{8,4},{12,8},{16,12},{20,16},{24,20},{28,24},{32,28},{36,32}... | collective-permute-start | bytes 196616 | tf_op jit(solution)/shard_map/ppermute | solution.py:25
  105.8 1.9 copy-start.14
  174.3 1.3 copy-start.1
  180.2 1.9 copy-start.7
  180.3 2.3 copy-start.6
  182.6 2.2 copy-start.5
  183.1 2.2 copy-start.4
  185.3 43.7 %copy-start.10 = (bf16[16,64,64]{2,1,0:T(8,128)(2,1)S(1)}, bf16[16,64,64]{2,1,0:T(8,128)(2,1)}, u32[]{:S(2)}) copy-start(bf16[16,64,64]{2,1,0:T(8,128)(2,1)} %copy-done.9) | copy-start | bytes 393220
  187.0 7.0 %collective-permute-start.1 = (f32[64,64]{1,0:T(8,128)S(1)}, f32[64,64]{1,0:T(8,128)S(1)}, u32[]{:S(2)}, u32[]{:S(2)}) collective-permute-start(f32[64,64]{1,0:T(8,128)S(1)} %fusion.86), channel_id=1, source_target_pairs={{0,8},{4,12},{8,0},{12,4},{16,24},{20,28},{24,16},{28,20},{32,40},... | collective-permute-start | bytes 49160 | tf_op jit(solution)/shard_map/ppermute | solution.py:12
  194.4 7.3 %collective-permute-start.2 = (f32[64,64]{1,0:T(8,128)S(1)}, f32[64,64]{1,0:T(8,128)S(1)}, u32[]{:S(2)}, u32[]{:S(2)}) collective-permute-start(f32[64,64]{1,0:T(8,128)S(1)} %fusion.82), channel_id=1, source_target_pairs={{0,16},{4,20},{8,24},{12,28},{16,0},{20,4},{24,8},{28,12},{32,48},... | collective-permute-start | bytes 49160 | tf_op jit(solution)/shard_map/ppermute | solution.py:12
  202.1 12.6 %collective-permute-start.3 = (f32[64,64]{1,0:T(8,128)S(1)}, f32[64,64]{1,0:T(8,128)S(1)}, u32[]{:S(2)}, u32[]{:S(2)}) collective-permute-start(f32[64,64]{1,0:T(8,128)S(1)} %fusion.78), channel_id=1, source_target_pairs={{0,32},{4,36},{8,40},{12,44},{16,48},{20,52},{24,56},{28,60},{32,0... | collective-permute-start | bytes 49160 | tf_op jit(solution)/shard_map/ppermute | solution.py:12
  215.0 20.4 %collective-permute-start.4 = (f32[64,64]{1,0:T(8,128)S(1)}, f32[64,64]{1,0:T(8,128)S(1)}, u32[]{:S(2)}, u32[]{:S(2)}) collective-permute-start(f32[64,64]{1,0:T(8,128)S(1)} %fusion.74), channel_id=1, source_target_pairs={{0,64},{4,68},{8,72},{12,76},{16,80},{20,84},{24,88},{28,92},{32,9... | collective-permute-start | bytes 49160 | tf_op jit(solution)/shard_map/ppermute | solution.py:12
  234.3 1.1 copy-start.2
  235.8 6.0 %collective-permute-start.5 = (f32[64,64]{1,0:T(8,128)S(1)}, f32[64,64]{1,0:T(8,128)S(1)}, u32[]{:S(2)}, u32[]{:S(2)}) collective-permute-start(f32[64,64]{1,0:T(8,128)S(1)} %fusion.70), channel_id=1, source_target_pairs={{0,128},{4,132},{8,136},{12,140},{16,144},{20,148},{24,152},{28,15... | collective-permute-start | bytes 49160 | tf_op jit(solution)/shard_map/ppermute | solution.py:12
  242.2 7.3 %collective-permute-start.6 = (f32[64,64]{1,0:T(8,128)S(1)}, f32[64,64]{1,0:T(8,128)S(1)}, u32[]{:S(2)}, u32[]{:S(2)}) collective-permute-start(f32[64,64]{1,0:T(8,128)S(1)} %fusion.66), channel_id=1, source_target_pairs={{0,256},{4,260},{8,264},{12,268},{16,272},{20,276},{24,280},{28,28... | collective-permute-start | bytes 49160 | tf_op jit(solution)/shard_map/ppermute | solution.py:12
  (2 other events, 1.7 us)
Sparse Core Ops, SparseCore 0:
  235.6 20.9 reduce-scatter.1
where the time goes:
time: 294 us; the launch traced here: 293 us
  other arithmetic  144 us (49%)
  starting transfers between devices  49.6 us (17%)
  matrix products  49.4 us (17%)
  local copies, waits for them, and re-layouts  18.1 us (6%)
  between operations  14.6 us (5%)
  waiting for transfers between devices  10.2 us (3%)
  loops' own time  7.09 us (2%)
    add x128, other arithmetic, column_step(): lower_part = lower_part + scaled_column[..., :, None] * marker  53.9 us
    ppermute x7, starting transfers between devices, swapped(): lax.ppermute(shard, axis, [(i, i ^ 1 << apart) for i in range(lax.axis_si...  45.1 us
    dot_general x64, matrix products, row_step(): jnp.einsum('...j,...jc->...c', earlier, solved, precision=highest_precision)  33.4 us
    reduce_sum x128, other arithmetic, column_step(): column_vals = jnp.sum(working * marker, axis=-1)  29.9 us
    reduce_sum x128, other arithmetic, column_step(): pivot_value = jnp.sum(column_vals * marker, axis=-1)  14.5 us
    ppermute x7, waiting for transfers between devices, swapped(): lax.ppermute(shard, axis, [(i, i ^ 1 << apart) for i in range(lax.axis_si...  10.2 us
    select_n x128, other arithmetic, column_step(): jnp.where(positions >= column, column_vals / jnp.sqrt(pivot_value)[..., N...  9.7 us
    add x64, other arithmetic, row_step(): return solved + marker[:, None] * new_row[..., None, :]  9.06 us
  transfers between devices with their start and end apart: 10, of which 5 were waited for; matrix products, arithmetic and copies ran while one was open for 68% of the time, Pallas kernels for 0%

commit v1 on v0

v1 whole, which is shorter than its diff:
```python
import functools
import math

import jax
import jax.numpy as jnp
from jax import lax
from jax.experimental import pallas as pl
from jax.experimental.pallas import tpu as pltpu
from jax.sharding import PartitionSpec as P

F32 = jnp.float32
BF16 = jnp.bfloat16
VMEM = pltpu.VMEM
SMEM = pltpu.SMEM


def split(x):
    high = x.astype(BF16)
    return high, (x - high.astype(F32)).astype(BF16)


def dot_nn(a, b):
    return lax.dot_general(a, b, (((1,), (0,)), ((), ())), preferred_element_type=F32)


def dot_nt(a, b):
    return lax.dot_general(a, b, (((1,), (1,)), ((), ())), preferred_element_type=F32)


def dot_tn(a, b):
    return lax.dot_general(a, b, (((0,), (0,)), ((), ())), preferred_element_type=F32)


def carry(move, gram):
    move_h, move_l = move
    gram_h, gram_l = split(gram)
    right = dot_nn(gram_h, move_h) + dot_nn(gram_l, move_h)
    if move_l is not None:
        right = right + dot_nn(gram_h, move_l)
    right_h, right_l = split(right)
    out = dot_tn(move_h, right_h) + dot_tn(move_h, right_l)
    if move_l is not None:
        out = out + dot_tn(move_l, right_h)
    return out


def panel_chain(panel, start):
    count, rows, _ = panel.shape
    sub = lax.broadcasted_iota(jnp.int32, (1, rows, 128), 1)
    scale = jnp.zeros((count, rows, 128), F32)
    for r in range(rows):
        col = jnp.broadcast_to(panel[:, :, start + r : start + r + 1], panel.shape)
        inv = lax.rsqrt(col[:, r : r + 1, :])
        outer = jnp.where(sub > r, col, 0.0) * panel[:, r : r + 1, :]
        panel = panel - outer * (inv * inv)
        scale = jnp.where(sub == r, inv, scale)
    return panel * scale


def panel_ahead(panel, start):
    count, rows, _ = panel.shape
    sub = lax.broadcasted_iota(jnp.int32, (1, rows, 128), 1)
    scale = jnp.zeros((count, rows, 128), F32)
    cols = [
        jnp.broadcast_to(panel[:, :, start + r : start + r + 1], panel.shape) for r in range(rows)
    ]
    for r in range(rows):
        inv = lax.rsqrt(cols[r][:, r : r + 1, :])
        mult = jnp.where(sub > r, cols[r], 0.0) * (inv * inv)
        panel = panel - mult * panel[:, r : r + 1, :]
        for t in range(r + 1, rows):
            cols[t] = cols[t] - mult * cols[t][:, r : r + 1, :]
        scale = jnp.where(sub == r, inv, scale)
    return panel * scale


def factor(work, done, first, count, rows, eliminate):
    size = work.shape[1]
    last = first + count
    for k in range(0, size, rows):
        panel = eliminate(work[first:last, k : k + rows, :], k)
        done[first:last, k : k + rows, :] = panel
        if k + rows < size:
            high, low = split(panel)
            left = jnp.concatenate([high, low, high], axis=1)
            right = jnp.concatenate([high, high, low], axis=1)
            for i in range(count):
                down = dot_tn(left[i], right[i])
                work[first + i, k + rows : size, :] = (
                    work[first + i, k + rows : size, :] - down[k + rows : size, :]
                )


def upper_mask(size):
    return lax.broadcasted_iota(jnp.int32, (size, size), 0) <= lax.broadcasted_iota(
        jnp.int32, (size, size), 1
    )


def eye(size):
    return (
        lax.broadcasted_iota(jnp.int32, (size, size), 0)
        == lax.broadcasted_iota(jnp.int32, (size, size), 1)
    ).astype(F32)


def tree_kernel(pairing, basis, leaf_move, inner_move, q_out, inner_out, root_out, low_out, work, done):
    leaves, size, panels = basis.shape
    inner = inner_move.shape[0]
    part = q_out.shape[2]
    identity = eye(size)
    for i in range(leaves + inner):
        work[i, :, size : 2 * size] = identity
    for i in range(leaves):
        work[i, :, 0:size] = dot_nt(basis[i], basis[i])
    for m in range(leaves // 2):
        a, b = pairing[0, 2 * m], pairing[0, 2 * m + 1]
        work[leaves + m, :, 0:size] = carry(split(leaf_move[a]), work[a, :, 0:size]) + carry(
            split(leaf_move[b]), work[b, :, 0:size]
        )
    below, count = 0, leaves // 2
    while count > 1:
        for m in range(count // 2):
            a = below + 2 * m
            work[leaves + below + count + m, :, 0:size] = carry(
                split(inner_move[a]), work[leaves + a, :, 0:size]
            ) + carry(split(inner_move[a + 1]), work[leaves + a + 1, :, 0:size])
        below, count = below + count, count // 2
    root_out[...] = carry(split(inner_move[inner - 1]), work[leaves + inner - 1, :, 0:size])
    factor(work, done, 0, leaves + inner, 16, panel_chain)
    keep = upper_mask(size)
    for i in range(inner):
        inner_out[i] = jnp.where(keep, done[leaves + i, :, 0:size], 0.0)
    begin = pl.multiple_of(lax.axis_index("blk") * part, part)
    for i in range(leaves):
        low_out[i] = jnp.where(keep, done[i, :, 0:size], 0.0).astype(BF16)
        weights = (math.sqrt(panels) * done[i, :, size : 2 * size]).astype(BF16)
        q_out[i] = dot_nn(weights, basis[i, :, pl.ds(begin, part)]).astype(BF16)


def pack(matrix):
    half = matrix.shape[0] // 2
    return jnp.concatenate([matrix[:half], matrix[half:]], axis=1)


def unpack(packed):
    half = packed.shape[1] // 2
    return jnp.concatenate([packed[:, :half], packed[:, half:]], axis=0)


def link_kernel(
    index,
    mask,
    root,
    moves,
    low,
    coupling,
    upper_out,
    projected,
    weight_out,
    extended,
    half_ref,
    send,
    recv,
    row_send,
    row_recv,
    work,
    done,
    send_sem,
    recv_sem,
    halo_send_sem,
    halo_recv_sem,
    row_send_sem,
    row_recv_sem,
):
    leaves, slots, size, _ = coupling.shape
    halo = leaves // 2
    n_leaf, blocks = lax.axis_size("leaf"), lax.axis_size("blk")
    me, blk = lax.axis_index("leaf"), lax.axis_index("blk")
    after, before = lax.rem(me + 1, n_leaf), lax.rem(me + n_leaf - 1, n_leaf)
    depth = upper_out.shape[0]

    def flipped(apart):
        out, bit = me, 1
        while bit <= apart:
            if apart & bit:
                out = out + bit - 2 * bit * lax.rem(out // bit, 2)
            bit *= 2
        return out

    groups = [(1,)] + [(2 << (2 * g), 4 << (2 * g), 6 << (2 * g)) for g in range((depth - 1) // 2)]
    barrier = pltpu.get_barrier_semaphore()
    total = 0
    for group in groups:
        for apart in group:
            pl.semaphore_signal(barrier, 1, device_id={"leaf": flipped(apart)})
            total += 1
    for peer in (after, before):
        pl.semaphore_signal(barrier, 1, device_id={"leaf": peer})
        total += 1
    for d in range(1, blocks):
        pl.semaphore_signal(barrier, 1, device_id={"blk": lax.rem(blk + d, blocks)})
        total += 1
    pl.semaphore_wait(barrier, total)

    slot_of, used = {}, [0, 0]

    def start_exchange(step, terms):
        firsts = []
        for term in terms:
            send[used[0]] = pack(term)
            firsts.append(used[0])
            used[0] += 1
        started = []
        for j, apart in enumerate(groups[step]):
            parts = firsts if j == 0 else firsts[-1:]
            for source in parts:
                at = used[1]
                used[1] += 1
                copy = pltpu.make_async_remote_copy(
                    src_ref=send.at[source],
                    dst_ref=recv.at[at],
                    send_sem=send_sem.at[at],
                    recv_sem=recv_sem.at[at],
                    device_id={"leaf": flipped(apart)},
                )
                copy.start()
                started.append((copy, source, at))
        return started

    def finish_exchange(started):
        sums = {}
        for copy, source, at in started:
            copy.wait_recv()
            sums[source] = sums.get(source, send[source]) + recv[at]
        return [unpack(sums[s]) for s in sorted(sums)]

    grams = []

    def next_terms(gram):
        level = len(grams)
        near = moves[level - 1]
        far = split(dot_nn(near, moves[level]))
        return [carry((near, None), gram), carry(far, gram)]

    going = [start_exchange(0, [root[...]])]
    for i in range(leaves):
        extended[halo + i] = low[i]
    halo_copies = []
    for j, (peer, source, target) in enumerate(
        ((after, halo + leaves - halo, 0), (before, halo, halo + leaves))
    ):
        copy = pltpu.make_async_remote_copy(
            src_ref=extended.at[pl.ds(source, halo)],
            dst_ref=extended.at[pl.ds(target, halo)],
            send_sem=halo_send_sem.at[j],
            recv_sem=halo_recv_sem.at[j],
            device_id={"leaf": peer},
        )
        copy.start()
        halo_copies.append(copy)

    for t in range(leaves):
        for s in range(slots):
            half_ref[t, s] = dot_nn(low[t], coupling[t, s]).astype(BF16)

    grams += finish_exchange(going[-1])
    going.append(start_exchange(1, next_terms(grams[-1])))
    for copy in halo_copies:
        copy.wait_recv()

    per = leaves // blocks
    base = me * leaves - halo
    row_scale = 1.0 / (slots * blocks * size)
    row_copies = []
    own_rows = []
    for d in range(1, blocks + 1):
        peer = lax.rem(blk + d, blocks)
        for i in range(per):
            t = peer * per + i
            rows = None
            for s in range(slots):
                source = jnp.clip(index[t, s] - base, 0, leaves + 2 * halo - 1)
                full = dot_nt(half_ref[t, s], extended[source])
                value = (full * mask[t, s].astype(F32)).astype(BF16)
                projected[t, s] = value
                term = dot_nt(value, value)
                rows = term if rows is None else rows + term
            if d < blocks:
                row_send[d - 1, i] = (rows * row_scale).astype(BF16)
            else:
                own_rows.append(rows * row_scale)
        if d < blocks:
            copy = pltpu.make_async_remote_copy(
                src_ref=row_send.at[d - 1],
                dst_ref=row_recv.at[d - 1],
                send_sem=row_send_sem.at[d - 1],
                recv_sem=row_recv_sem.at[d - 1],
                device_id={"blk": peer},
            )
            copy.start()
            row_copies.append(copy)
        if d < len(groups) - 1:
            grams += finish_exchange(going[-1])
            going.append(start_exchange(d + 1, next_terms(grams[-1])))
    for copy in row_copies:
        copy.wait_recv()
    for i in range(per):
        rows = own_rows[i]
        for d in range(blocks - 1):
            rows = rows + row_recv[d, i].astype(F32)
        weight_out[i] = rows
    grams += finish_exchange(going[-1])

    for i in range(depth):
        work[i, :, 0:size] = grams[i]
        work[i, :, size : 2 * size] = jnp.zeros((size, size), F32)
    factor(work, done, 0, depth, 8, panel_ahead)
    keep = upper_mask(size)
    for i in range(depth):
        upper_out[i] = jnp.where(keep, done[i, :, 0:size], 0.0)
    for started in going:
        for copy, _, _ in started:
            copy.wait_send()
    for copy in halo_copies + row_copies:
        copy.wait_send()


def local(
    leaf_basis,
    leaf_pairing,
    leaf_transfer,
    inner_transfer,
    upper_transfer,
    coupling,
    source_cluster_index,
    coupling_slot_mask,
):
    leaves, size, panels = leaf_basis.shape
    inner = inner_transfer.shape[1]
    n_leaf, blocks = lax.axis_size("leaf"), lax.axis_size("blk")
    depth = n_leaf.bit_length() - 1
    slots = coupling.shape[1]
    part = panels // blocks
    vmem = pl.BlockSpec(memory_space=VMEM)
    smem = pl.BlockSpec(memory_space=SMEM)

    q, inner_factor, root, low = pl.pallas_call(
        tree_kernel,
        out_shape=(
            jax.ShapeDtypeStruct((leaves, size, part), BF16),
            jax.ShapeDtypeStruct((inner, size, size), F32),
            jax.ShapeDtypeStruct((size, size), F32),
            jax.ShapeDtypeStruct((leaves, size, size), BF16),
        ),
        in_specs=[smem, vmem, vmem, vmem],
        out_specs=(vmem,) * 4,
        scratch_shapes=[
            VMEM((leaves + inner, size, 2 * size), F32),
            VMEM((leaves + inner, size, 2 * size), F32),
        ],
        compiler_params=pltpu.CompilerParams(vmem_limit_bytes=40 * 2**20),
    )(leaf_pairing, leaf_basis, leaf_transfer, inner_transfer[0])

    me = lax.axis_index("leaf")
    level = jnp.arange(1, depth, dtype=jnp.int32)
    owner = (me >> level << level) + (1 << (level - 1))
    choose = (owner[:, None] == jnp.arange(n_leaf, dtype=jnp.int32)[None, :]).astype(BF16)
    moves = jnp.einsum("rn,nba->rba", choose, upper_transfer, preferred_element_type=F32).astype(
        BF16
    )

    n_recv = 1 + 4 * ((depth - 1) // 2)
    n_send = 1 + 2 * ((depth - 1) // 2)
    upper_factor, projected, row_weight = pl.pallas_call(
        link_kernel,
        out_shape=(
            jax.ShapeDtypeStruct((depth, size, size), F32),
            jax.ShapeDtypeStruct(coupling.shape, BF16),
            jax.ShapeDtypeStruct((leaves // blocks, size, size), F32),
        ),
        in_specs=[smem, smem, vmem, vmem, vmem, vmem],
        out_specs=(vmem,) * 3,
        scratch_shapes=[
            VMEM((2 * leaves, size, size), BF16),
            VMEM((leaves, slots, size, size), BF16),
            VMEM((n_send, size // 2, 2 * size), F32),
            VMEM((n_recv, size // 2, 2 * size), F32),
            VMEM((blocks - 1, leaves // blocks, size, size), BF16),
            VMEM((blocks - 1, leaves // blocks, size, size), BF16),
            VMEM((depth, size, 2 * size), F32),
            VMEM((depth, size, 2 * size), F32),
            pltpu.SemaphoreType.DMA((n_recv,)),
            pltpu.SemaphoreType.DMA((n_recv,)),
            pltpu.SemaphoreType.DMA((2,)),
            pltpu.SemaphoreType.DMA((2,)),
            pltpu.SemaphoreType.DMA((blocks - 1,)),
            pltpu.SemaphoreType.DMA((blocks - 1,)),
        ],
        compiler_params=pltpu.CompilerParams(
            collective_id=0, has_side_effects=True, vmem_limit_bytes=40 * 2**20
        ),
    )(source_cluster_index, coupling_slot_mask, root, moves, low, coupling)
    return (q, inner_factor[None], upper_factor[None], projected, row_weight)


def solution(mesh):
    placed = (
        P("leaf", None, None),
        P("leaf", None),
        P("leaf", None, None),
        P("leaf", None, None, None),
        P(),
        P("leaf", "blk", None, None),
        P("leaf", "blk"),
        P("leaf", "blk"),
    )
    return jax.shard_map(
        local,
        mesh=mesh,
        in_specs=placed,
        out_specs=(
            P("leaf", None, "blk"),
            P("leaf", None, None, None),
            P("leaf", None, None, None),
            P("leaf", "blk", None, None),
            P(("leaf", "blk"), None, None),
        ),
        check_vma=False,
    )
```

time: 294 us -> 61.1 us (0.21)
  other arithmetic: 144 us -> 0.01 us
  Pallas kernels: 0 us -> 52.5 us
  starting transfers between devices: 49.6 us -> 0 us
  matrix products: 49.4 us -> 0.91 us
  between operations: 14.6 us -> 0.69 us
  local copies, waits for them, and re-layouts: 18.1 us -> 6.74 us
  waiting for transfers between devices: 10.2 us -> 0 us
  loops' own time: 7.09 us -> 0 us
    add x192 -> x1, other arithmetic: 63 us -> 0.01 us  [local(): owner = (me >> level << level) + (1 << level - 1)]
    reduce_sum x384 -> x0, other arithmetic: 60.7 us -> none  [the longest x128 29.9 us: column_step(): column_vals = jnp.sum(working * marker, axis=-1)]
    pallas_call x0 -> x2, Pallas kernels: none -> 52.5 us  [the longest x1 39 us: local(): pl.pallas_call(link_kernel, out_shape=(jax.ShapeDtypeStruct((depth, size,...]
    ppermute x9 -> x0, starting transfers between devices: 49.6 us -> none  [the longest x7 45.1 us: swapped(): lax.ppermute(shard, axis, [(i, i ^ 1 << apart) for i in range(lax.axis_si...]
    dot_general x93 -> x1, matrix products: 49.4 us -> 0.91 us  [local(): jnp.einsum('rn,nba->rba', choose, upper_transfer, preferred_element_type=...]
    ppermute x9 -> x0, waiting for transfers between devices: 10.2 us -> none  [the longest x7 10.2 us: swapped(): lax.ppermute(shard, axis, [(i, i ^ 1 << apart) for i in range(lax.axis_si...]
    select_n x128 -> x0, other arithmetic: 9.7 us -> none  [column_step(): jnp.where(positions >= column, column_vals / jnp.sqrt(pivot_value)[..., N...]
    another operation x3 -> x0, loops' own time: 7.09 us -> none  [the longest x2 4.87 us: triangle_of(): lax.fori_loop(0, order_size, column_step, (gram_in, start_lower))]
  transfers between devices with their start and end apart: 10 -> 0, of which waited for: 5 -> 0; matrix products, arithmetic and copies ran while one was open for 68% -> 0% of each run, Pallas kernels for 0% -> 0%
where the time goes in v1:
time: 61.1 us; the launch traced here: 60.9 us
  Pallas kernels  52.5 us (86%)
  local copies, waits for them, and re-layouts  6.74 us (11%)
  matrix products  0.91 us (1%)
  between operations  0.69 us (1%)
    pallas_call x1, Pallas kernels, local(): pl.pallas_call(link_kernel, out_shape=(jax.ShapeDtypeStruct((depth, size,...  39 us
    pallas_call x1, Pallas kernels, local(): pl.pallas_call(tree_kernel, out_shape=(jax.ShapeDtypeStruct((leaves, size...  13.5 us
    unnamed x17, local copies, waits for them, and re-layouts  6.69 us

profile of v1, /device:TPU:6, one launch (start us, length us, event | category | flops | bytes accessed | tf_op | source)
XLA Modules:
  0.0 60.9 jit_solution(5198159490878670055)
XLA Ops:
  0.6 0.0 copy-start
  0.6 0.0 copy-start.1
  0.7 0.9 %copy.14.index = s32[16,4]{1,0:T(8,128)S(1)} copy(s32[16,4]{0,1:T(4,128)} %param.14) | data formatting | bytes 512 | tf_op args[6]
  1.6 0.8 %copy.15.mask = s32[16,4]{1,0:T(8,128)S(1)} copy(s32[16,4]{0,1:T(4,128)} %param.15) | data formatting | bytes 512 | tf_op args[7]
  2.3 0.0 copy-done
  2.3 0.9 %fusion.1 = bf16[6,64,64]{2,0,1:T(8,128)(2,1)S(1)} fusion(bf16[128,64,64]{0,2,1:T(8,128)(2,1)S(1)} %copy-done, s32[6]{0:T(128)S(1)} %fusion.4), kind=kOutput, calls=%fused_computation.3 | convolution fusion | flops 6292224 | bytes 1097752 | tf_op jit(solution)/shard_map/rn,nba->rba/dot_general | solution.py:369
  3.2 0.0 copy-start.5
  3.3 0.0 copy-done.1
  3.3 0.6 %copy-done.5 = s32[1,16]{1,0:T(1,128)S(1)} copy-done((s32[1,16]{1,0:T(1,128)S(1)}, s32[1,16]{1,0:T(1,128)}, u32[]{:S(2)}) %copy-start.5) | copy-done | bytes 88
  3.9 0.0 copy-start.3
  3.9 1.0 %copy-done.3 = f32[16,64,64]{2,1,0:T(8,128)S(1)} copy-done((f32[16,64,64]{2,1,0:T(8,128)S(1)}, f32[16,64,64]{2,1,0:T(8,128)}, u32[]{:S(2)}) %copy-start.3) | copy-done | bytes 262168
  5.0 0.0 copy-start.4
  5.0 1.0 %copy-done.4 = f32[1,15,64,64]{3,2,1,0:T(8,128)S(1)} copy-done((f32[1,15,64,64]{3,2,1,0:T(8,128)S(1)}, f32[1,15,64,64]{3,2,1,0:T(8,128)}, u32[]{:S(2)}) %copy-start.4) | copy-done | bytes 245784
  6.0 0.0 copy-start.2
  6.0 13.5 %shard_map.119 = (bf16[16,64,128]{2,1,0:T(8,128)(2,1)}, f32[15,64,64]{2,1,0:T(8,128)}, f32[64,64]{1,0:T(8,128)S(1)}, bf16[16,64,64]{2,1,0:T(8,128)(2,1)S(1)}) custom-call(s32[1,16]{1,0:T(1,128)S(1)} %copy-done.5, bf16[16,64,512]{2,1,0:T(8,128)(2,1)S(1)} %copy-done.1, f32[16,64,64]{2,1,0:T(8,128)S(1)} %copy-done.3, f32[15,64,64]{2,1,0:T(8,128)S(1)} %bitcast.7), custom_call_target="tpu_custom_call" | custom-call | tf_op jit(solution)/shard_map/pallas_call | solution.py:348
  19.5 0.0 copy-done.2
  19.6 39.0 %shard_map.120 = (f32[7,64,64]{2,1,0:T(8,128)S(1)}, bf16[16,4,64,64]{3,2,1,0:T(8,128)(2,1)S(1)}, f32[4,64,64]{2,1,0:T(8,128)S(1)}) custom-call(s32[16,4]{1,0:T(8,128)S(1)} %copy.14.index, s32[16,4]{1,0:T(8,128)S(1)} %copy.15.mask, f32[64,64]{1,0:T(8,128)S(1)} %get-tuple-element.14.root, bf16[6,64,64]{2,1,0:T(8,128)(2,1)S(1)} %copy.17.moves, ...), custom_call_target="tpu_custom_call" | custom-call | tf_op jit(solution)/shard_map/pallas_call | solution.py:375
  58.5 0.7 %copy.21 = f32[1,7,64,64]{3,2,1,0:T(8,128)} copy(f32[1,7,64,64]{3,2,1,0:T(8,128)S(1)} %bitcast.8) | data formatting | bytes 229376
  59.2 1.0 %copy.22 = bf16[16,4,64,64]{3,2,1,0:T(8,128)(2,1)} copy(bf16[16,4,64,64]{3,2,1,0:T(8,128)(2,1)S(1)} %get-tuple-element.27) | data formatting | bytes 1048576
  60.2 0.7 %copy.23 = f32[4,64,64]{2,1,0:T(8,128)} copy(f32[4,64,64]{2,1,0:T(8,128)S(1)} %get-tuple-element.28) | data formatting | bytes 131072
  (2 shorter events, 0.1 us)
Async XLA Ops:
  0.6 1.7 %copy-start = (bf16[128,64,64]{0,2,1:T(8,128)(2,1)S(1)}, bf16[128,64,64]{0,2,1:T(8,128)(2,1)}, u32[]{:S(2)}) copy-start(bf16[128,64,64]{0,2,1:T(8,128)(2,1)} %param.12) | copy-start | bytes 3145732
  0.6 2.7 %copy-start.1 = (bf16[16,64,512]{2,1,0:T(8,128)(2,1)S(1)}, bf16[16,64,512]{2,1,0:T(8,128)(2,1)}, u32[]{:S(2)}) copy-start(bf16[16,64,512]{2,1,0:T(8,128)(2,1)} %basis.1) | copy-start | bytes 3145732
  3.2 0.7 %copy-start.5 = (s32[1,16]{1,0:T(1,128)S(1)}, s32[1,16]{1,0:T(1,128)}, u32[]{:S(2)}) copy-start(s32[1,16]{1,0:T(1,128)} %pairing.1) | copy-start | bytes 196
  3.9 1.0 %copy-start.3 = (f32[16,64,64]{2,1,0:T(8,128)S(1)}, f32[16,64,64]{2,1,0:T(8,128)}, u32[]{:S(2)}) copy-start(f32[16,64,64]{2,1,0:T(8,128)} %leaf_move.1) | copy-start | bytes 786436
  5.0 1.0 %copy-start.4 = (f32[1,15,64,64]{3,2,1,0:T(8,128)S(1)}, f32[1,15,64,64]{3,2,1,0:T(8,128)}, u32[]{:S(2)}) copy-start(f32[1,15,64,64]{3,2,1,0:T(8,128)} %param.11) | copy-start | bytes 737284
  6.0 13.5 %copy-start.2 = (bf16[16,4,64,64]{3,2,1,0:T(8,128)(2,1)S(1)}, bf16[16,4,64,64]{3,2,1,0:T(8,128)(2,1)}, u32[]{:S(2)}) copy-start(bf16[16,4,64,64]{3,2,1,0:T(8,128)(2,1)} %coupling.1) | copy-start | bytes 1572868

commit v2 on v1

v2 whole, which is shorter than its diff:
```python
import functools
import math

import jax
import jax.numpy as jnp
from jax import lax
from jax.experimental import pallas as pl
from jax.experimental.pallas import tpu as pltpu
from jax.sharding import PartitionSpec as P

F32 = jnp.float32
BF16 = jnp.bfloat16
VMEM = pltpu.VMEM
SMEM = pltpu.SMEM


def split(x):
    high = x.astype(BF16)
    return high, (x - high.astype(F32)).astype(BF16)


def dot_nn(a, b):
    return lax.dot_general(a, b, (((1,), (0,)), ((), ())), preferred_element_type=F32)


def dot_nt(a, b):
    return lax.dot_general(a, b, (((1,), (1,)), ((), ())), preferred_element_type=F32)


def dot_tn(a, b):
    return lax.dot_general(a, b, (((0,), (0,)), ((), ())), preferred_element_type=F32)


def carry(move, gram):
    move_h, move_l = move
    gram_h, gram_l = split(gram)
    right = dot_nn(gram_h, move_h) + dot_nn(gram_l, move_h)
    if move_l is not None:
        right = right + dot_nn(gram_h, move_l)
    right_h, right_l = split(right)
    out = dot_tn(move_h, right_h) + dot_tn(move_h, right_l)
    if move_l is not None:
        out = out + dot_tn(move_l, right_h)
    return out


def panel_chain(panel, start):
    count, rows, _ = panel.shape
    sub = lax.broadcasted_iota(jnp.int32, (1, rows, 128), 1)
    scale = jnp.zeros((count, rows, 128), F32)
    for r in range(rows):
        col = jnp.broadcast_to(panel[:, :, start + r : start + r + 1], panel.shape)
        inv = lax.rsqrt(col[:, r : r + 1, :])
        outer = jnp.where(sub > r, col, 0.0) * panel[:, r : r + 1, :]
        panel = panel - outer * (inv * inv)
        scale = jnp.where(sub == r, inv, scale)
    return panel * scale


def panel_ahead(panel, start):
    count, rows, _ = panel.shape
    sub = lax.broadcasted_iota(jnp.int32, (1, rows, 128), 1)
    scale = jnp.zeros((count, rows, 128), F32)
    cols = [
        jnp.broadcast_to(panel[:, :, start + r : start + r + 1], panel.shape) for r in range(rows)
    ]
    for r in range(rows):
        inv = lax.rsqrt(cols[r][:, r : r + 1, :])
        mult = jnp.where(sub > r, cols[r], 0.0) * (inv * inv)
        panel = panel - mult * panel[:, r : r + 1, :]
        for t in range(r + 1, rows):
            cols[t] = cols[t] - mult * cols[t][:, r : r + 1, :]
        scale = jnp.where(sub == r, inv, scale)
    return panel * scale


def factor_panel(work, done, first, count, rows, k, eliminate):
    size = work.shape[1]
    last = first + count
    panel = eliminate(work[first:last, k : k + rows, :], k)
    done[first:last, k : k + rows, :] = panel
    if k + rows < size:
        high, low = split(panel)
        left = jnp.concatenate([high, low, high], axis=1)
        right = jnp.concatenate([high, high, low], axis=1)
        for i in range(count):
            down = dot_tn(left[i], right[i])
            work[first + i, k + rows : size, :] = (
                work[first + i, k + rows : size, :] - down[k + rows : size, :]
            )


def upper_mask(size):
    return lax.broadcasted_iota(jnp.int32, (size, size), 0) <= lax.broadcasted_iota(
        jnp.int32, (size, size), 1
    )


def eye(size):
    return (
        lax.broadcasted_iota(jnp.int32, (size, size), 0)
        == lax.broadcasted_iota(jnp.int32, (size, size), 1)
    ).astype(F32)


def pack(matrix):
    half = matrix.shape[0] // 2
    return jnp.concatenate([matrix[:half], matrix[half:]], axis=1)


def unpack(packed):
    half = packed.shape[1] // 2
    return jnp.concatenate([packed[:, :half], packed[:, half:]], axis=0)


def tree_kernel(
    pairing_hbm,
    basis_hbm,
    leaf_move_hbm,
    inner_move_hbm,
    moves_hbm,
    coupling_hbm,
    index_hbm,
    mask_hbm,
    q_hbm,
    inner_hbm,
    gram_hbm,
    projected_hbm,
    weight_hbm,
    q_out,
    inner_out,
    gram_out,
    projected,
    weight_out,
    pairing,
    basis,
    leaf_move,
    inner_move,
    moves,
    coupling,
    index,
    mask,
    work,
    done,
    extended,
    half_ref,
    send,
    recv,
    row_send,
    row_recv,
    in_sem,
    out_sem,
    send_sem,
    recv_sem,
    halo_send_sem,
    halo_recv_sem,
    row_send_sem,
    row_recv_sem,
):
    leaves, size, panels = basis.shape
    inner = inner_move.shape[0]
    slots = coupling.shape[1]
    part = q_out.shape[2]
    halo = leaves // 2
    n_leaf, blocks = lax.axis_size("leaf"), lax.axis_size("blk")
    me, blk = lax.axis_index("leaf"), lax.axis_index("blk")
    after, before = lax.rem(me + 1, n_leaf), lax.rem(me + n_leaf - 1, n_leaf)
    depth = gram_out.shape[0]

    loads = []
    for j, (source, target) in enumerate(
        (
            (basis_hbm, basis),
            (pairing_hbm, pairing),
            (leaf_move_hbm, leaf_move),
            (inner_move_hbm, inner_move),
            (moves_hbm, moves),
            (coupling_hbm, coupling),
            (index_hbm, index),
            (mask_hbm, mask),
        )
    ):
        load = pltpu.make_async_copy(source, target, in_sem.at[j])
        load.start()
        loads.append(load)

    stores = []

    def store_out(source, target):
        store = pltpu.make_async_copy(source, target, out_sem.at[len(stores)])
        store.start()
        stores.append(store)

    def flipped(apart):
        out, bit = me, 1
        while bit <= apart:
            if apart & bit:
                out = out + bit - 2 * bit * lax.rem(out // bit, 2)
            bit *= 2
        return out

    groups = [(1,)] + [(2 << (2 * g), 4 << (2 * g), 6 << (2 * g)) for g in range((depth - 1) // 2)]
    barrier = pltpu.get_barrier_semaphore()
    total = 0
    for group in groups:
        for apart in group:
            pl.semaphore_signal(barrier, 1, device_id={"leaf": flipped(apart)})
            total += 1
    for peer in (after, before):
        pl.semaphore_signal(barrier, 1, device_id={"leaf": peer})
        total += 1
    for d in range(1, blocks):
        pl.semaphore_signal(barrier, 1, device_id={"blk": lax.rem(blk + d, blocks)})
        total += 1

    used = [0, 0]

    def start_exchange(step, terms):
        firsts = []
        for term in terms:
            send[used[0]] = pack(term)
            firsts.append(used[0])
            used[0] += 1
        started = []
        for j, apart in enumerate(groups[step]):
            parts = firsts if j == 0 else firsts[-1:]
            for source in parts:
                at = used[1]
                used[1] += 1
                copy = pltpu.make_async_remote_copy(
                    src_ref=send.at[source],
                    dst_ref=recv.at[at],
                    send_sem=send_sem.at[at],
                    recv_sem=recv_sem.at[at],
                    device_id={"leaf": flipped(apart)},
                )
                copy.start()
                started.append((copy, source, at))
        return started

    def finish_exchange(started):
        sums = {}
        for copy, source, at in started:
            copy.wait_recv()
            sums[source] = sums.get(source, send[source]) + recv[at]
        return [unpack(sums[s]) for s in sorted(sums)]

    grams, going = [], []

    def advance():
        grams.extend(finish_exchange(going[-1]))
        if len(going) < len(groups):
            level = len(grams)
            near = moves[level - 1]
            far = split(dot_nn(near, moves[level]))
            terms = [carry((near, None), grams[-1]), carry(far, grams[-1])]
            going.append(start_exchange(len(going), terms))

    identity = eye(size)
    for i in range(leaves + inner):
        work[i, :, size : 2 * size] = identity
    loads[0].wait()
    for i in range(leaves):
        work[i, :, 0:size] = dot_nt(basis[i], basis[i])
    for j in (1, 2, 3):
        loads[j].wait()
    for m in range(leaves // 2):
        a, b = pairing[0, 2 * m], pairing[0, 2 * m + 1]
        work[leaves + m, :, 0:size] = carry(split(leaf_move[a]), work[a, :, 0:size]) + carry(
            split(leaf_move[b]), work[b, :, 0:size]
        )
    below, count = 0, leaves // 2
    while count > 1:
        for m in range(count // 2):
            a = below + 2 * m
            work[leaves + below + count + m, :, 0:size] = carry(
                split(inner_move[a]), work[leaves + a, :, 0:size]
            ) + carry(split(inner_move[a + 1]), work[leaves + a + 1, :, 0:size])
        below, count = below + count, count // 2
    root = carry(split(inner_move[inner - 1]), work[leaves + inner - 1, :, 0:size])
    pl.semaphore_wait(barrier, total)
    going.append(start_exchange(0, [root]))
    for j in (4, 5, 6, 7):
        loads[j].wait()

    rows = 16
    for k in range(0, size, rows):
        factor_panel(work, done, 0, leaves + inner, rows, k, panel_chain)
        if k + rows < size:
            advance()

    keep = upper_mask(size)
    for i in range(leaves):
        extended[halo + i] = jnp.where(keep, done[i, :, 0:size], 0.0).astype(BF16)
    halo_copies = []
    for j, (peer, source, target) in enumerate(((after, leaves, 0), (before, halo, halo + leaves))):
        copy = pltpu.make_async_remote_copy(
            src_ref=extended.at[pl.ds(source, halo)],
            dst_ref=extended.at[pl.ds(target, halo)],
            send_sem=halo_send_sem.at[j],
            recv_sem=halo_recv_sem.at[j],
            device_id={"leaf": peer},
        )
        copy.start()
        halo_copies.append(copy)

    for t in range(leaves):
        for s in range(slots):
            half_ref[t, s] = dot_nn(extended[halo + t], coupling[t, s]).astype(BF16)
    begin = pl.multiple_of(blk * part, part)
    for i in range(leaves):
        weights = (math.sqrt(panels) * done[i, :, size : 2 * size]).astype(BF16)
        q_out[i] = dot_nn(weights, basis[i, :, pl.ds(begin, part)]).astype(BF16)
    for i in range(inner):
        inner_out[i] = jnp.where(keep, done[leaves + i, :, 0:size], 0.0)
    store_out(q_out, q_hbm)
    store_out(inner_out, inner_hbm)

    for copy in halo_copies:
        copy.wait_recv()
    per = leaves // blocks
    base = me * leaves - halo
    row_scale = 1.0 / (slots * blocks * size)
    row_copies = []
    own_rows = []
    for d in range(1, blocks + 1):
        peer = lax.rem(blk + d, blocks)
        for i in range(per):
            t = peer * per + i
            square = None
            for s in range(slots):
                source = jnp.clip(index[s, t] - base, 0, leaves + 2 * halo - 1)
                full = dot_nt(half_ref[t, s], extended[source])
                value = (full * mask[s, t].astype(F32)).astype(BF16)
                projected[t, s] = value
                term = dot_nt(value, value)
                square = term if square is None else square + term
            if d < blocks:
                row_send[d - 1, i] = (square * row_scale).astype(BF16)
            else:
                own_rows.append(square * row_scale)
        if d < blocks:
            copy = pltpu.make_async_remote_copy(
                src_ref=row_send.at[d - 1],
                dst_ref=row_recv.at[d - 1],
                send_sem=row_send_sem.at[d - 1],
                recv_sem=row_recv_sem.at[d - 1],
                device_id={"blk": peer},
            )
            copy.start()
            row_copies.append(copy)
    store_out(projected, projected_hbm)
    advance()
    for i in range(depth):
        gram_out[i] = grams[i]
    store_out(gram_out, gram_hbm)
    for copy in row_copies:
        copy.wait_recv()
    for i in range(per):
        square = own_rows[i]
        for d in range(blocks - 1):
            square = square + row_recv[d, i].astype(F32)
        weight_out[i] = square
    store_out(weight_out, weight_hbm)
    for started in going:
        for copy, _, _ in started:
            copy.wait_send()
    for copy in halo_copies + row_copies:
        copy.wait_send()
    for store in stores:
        store.wait()


def last_kernel(
    gram, q, inner, projected, weight, upper_out, q_out, inner_out, projected_out, weight_out, work, done, sem
):
    depth, size, _ = gram.shape
    stores = []
    for j, (source, target) in enumerate(
        ((projected, projected_out), (q, q_out), (inner, inner_out), (weight, weight_out))
    ):
        store = pltpu.make_async_copy(source, target, sem.at[j])
        store.start()
        stores.append(store)
    for i in range(depth):
        work[i, :, 0:size] = gram[i]
        work[i, :, size : 2 * size] = jnp.zeros((size, size), F32)
    rows = 8
    for k in range(0, size, rows):
        factor_panel(work, done, 0, depth, rows, k, panel_ahead)
    keep = upper_mask(size)
    for i in range(depth):
        upper_out[i] = jnp.where(keep, done[i, :, 0:size], 0.0)
    for store in stores:
        store.wait()


def local(
    leaf_basis,
    leaf_pairing,
    leaf_transfer,
    inner_transfer,
    upper_transfer,
    coupling,
    source_cluster_index,
    coupling_slot_mask,
):
    leaves, size, panels = leaf_basis.shape
    inner = inner_transfer.shape[1]
    n_leaf, blocks = lax.axis_size("leaf"), lax.axis_size("blk")
    depth = n_leaf.bit_length() - 1
    slots = coupling.shape[1]
    part = panels // blocks
    vmem = pl.BlockSpec(memory_space=VMEM)
    anywhere = pl.BlockSpec(memory_space=pl.ANY)

    me = lax.axis_index("leaf")
    level = jnp.arange(1, depth, dtype=jnp.int32)
    owner = (me >> level << level) + (1 << (level - 1))
    choose = (owner[:, None] == jnp.arange(n_leaf, dtype=jnp.int32)[None, :]).astype(BF16)
    moves = jnp.einsum("rn,nba->rba", choose, upper_transfer, preferred_element_type=F32).astype(
        BF16
    )

    n_recv = 1 + 4 * ((depth - 1) // 2)
    n_send = 1 + 2 * ((depth - 1) // 2)
    q_shape = jax.ShapeDtypeStruct((leaves, size, part), BF16)
    inner_shape = jax.ShapeDtypeStruct((inner, size, size), F32)
    upper_shape = jax.ShapeDtypeStruct((depth, size, size), F32)
    projected_shape = jax.ShapeDtypeStruct(coupling.shape, BF16)
    weight_shape = jax.ShapeDtypeStruct((leaves // blocks, size, size), F32)
    q, inner_factor, upper_gram, projected, row_weight = pl.pallas_call(
        tree_kernel,
        out_shape=(q_shape, inner_shape, upper_shape, projected_shape, weight_shape),
        in_specs=[anywhere] * 8,
        out_specs=(anywhere,) * 5,
        scratch_shapes=[
            VMEM(q_shape.shape, BF16),
            VMEM(inner_shape.shape, F32),
            VMEM(upper_shape.shape, F32),
            VMEM(coupling.shape, BF16),
            VMEM(weight_shape.shape, F32),
            SMEM((1, leaves), jnp.int32),
            VMEM((leaves, size, panels), BF16),
            VMEM((leaves, size, size), F32),
            VMEM((inner, size, size), F32),
            VMEM((depth - 1, size, size), BF16),
            VMEM(coupling.shape, BF16),
            SMEM((slots, leaves), jnp.int32),
            SMEM((slots, leaves), jnp.int32),
            VMEM((leaves + inner, size, 2 * size), F32),
            VMEM((leaves + inner, size, 2 * size), F32),
            VMEM((2 * leaves, size, size), BF16),
            VMEM((leaves, slots, size, size), BF16),
            VMEM((n_send, size // 2, 2 * size), F32),
            VMEM((n_recv, size // 2, 2 * size), F32),
            VMEM((blocks - 1, leaves // blocks, size, size), BF16),
            VMEM((blocks - 1, leaves // blocks, size, size), BF16),
            pltpu.SemaphoreType.DMA((8,)),
            pltpu.SemaphoreType.DMA((5,)),
            pltpu.SemaphoreType.DMA((n_recv,)),
            pltpu.SemaphoreType.DMA((n_recv,)),
            pltpu.SemaphoreType.DMA((2,)),
            pltpu.SemaphoreType.DMA((2,)),
            pltpu.SemaphoreType.DMA((blocks - 1,)),
            pltpu.SemaphoreType.DMA((blocks - 1,)),
        ],
        compiler_params=pltpu.CompilerParams(
            collective_id=0, has_side_effects=True, vmem_limit_bytes=60 * 2**20
        ),
    )(
        leaf_pairing,
        leaf_basis,
        leaf_transfer,
        inner_transfer[0],
        moves,
        coupling,
        source_cluster_index.T,
        coupling_slot_mask.T,
    )

    upper_factor, q, inner_factor, projected, row_weight = pl.pallas_call(
        last_kernel,
        out_shape=(upper_shape, q_shape, inner_shape, projected_shape, weight_shape),
        in_specs=[vmem] + [anywhere] * 4,
        out_specs=(vmem,) + (anywhere,) * 4,
        scratch_shapes=[
            VMEM((depth, size, 2 * size), F32),
            VMEM((depth, size, 2 * size), F32),
            pltpu.SemaphoreType.DMA((4,)),
        ],
        compiler_params=pltpu.CompilerParams(vmem_limit_bytes=60 * 2**20),
    )(upper_gram, q, inner_factor, projected, row_weight)
    return (q, inner_factor[None], upper_factor[None], projected, row_weight)


def solution(mesh):
    placed = (
        P("leaf", None, None),
        P("leaf", None),
        P("leaf", None, None),
        P("leaf", None, None, None),
        P(),
        P("leaf", "blk", None, None),
        P("leaf", "blk"),
        P("leaf", "blk"),
    )
    return jax.shard_map(
        local,
        mesh=mesh,
        in_specs=placed,
        out_specs=(
            P("leaf", None, "blk"),
            P("leaf", None, None, None),
            P("leaf", None, None, None),
            P("leaf", "blk", None, None),
            P(("leaf", "blk"), None, None),
        ),
        check_vma=False,
    )
```

time: 61.1 us -> 108 us (1.77); the launches traced: 60.9 us -> 106 us
  Pallas kernels: 52.5 us -> 103 us
  local copies, waits for them, and re-layouts: 6.74 us -> 1.9 us
    pallas_call x2, Pallas kernels: 52.5 us -> 103 us  [the longest x1 61.3 us: local(): pl.pallas_call(last_kernel, out_shape=(upper_shape, q_shape, inner_shape,...]
    unnamed x17 -> x2, local copies, waits for them, and re-layouts: 6.69 us -> 1.21 us
where the time goes in v2:
time: 108 us; the launch traced here: 106 us
  Pallas kernels  103 us (95%)
  local copies, waits for them, and re-layouts  1.9 us (2%)
    pallas_call x1, Pallas kernels, local(): pl.pallas_call(last_kernel, out_shape=(upper_shape, q_shape, inner_shape,...  61.3 us
    pallas_call x1, Pallas kernels, local(): pl.pallas_call(tree_kernel, out_shape=(q_shape, inner_shape, upper_shape,...  41.4 us

profile of v2, /device:TPU:6, one launch (start us, length us, event | category | flops | bytes accessed | tf_op | source)
XLA Modules:
  0.0 106.3 jit_solution(2823642883006263157)
XLA Ops:
  0.6 0.0 copy-start
  0.7 1.2 %copy-done = bf16[128,64,64]{0,2,1:T(8,128)(2,1)S(1)} copy-done((bf16[128,64,64]{0,2,1:T(8,128)(2,1)S(1)}, bf16[128,64,64]{0,2,1:T(8,128)(2,1)}, u32[]{:S(2)}) %copy-start) | copy-done | bytes 1048600
  1.9 0.9 fusion.1
  2.8 0.7 copy.15.moves_hbm
  3.5 41.4 %shard_map.119 = (bf16[16,64,128]{2,1,0:T(8,128)(2,1)}, f32[15,64,64]{2,1,0:T(8,128)}, f32[7,64,64]{2,1,0:T(8,128)}, bf16[16,4,64,64]{3,2,1,0:T(8,128)(2,1)}, f32[4,64,64]{2,1,0:T(8,128)}) custom-call(s32[1,16]{1,0:T(1,128)} %pairing_hbm.1, bf16[16,64,512]{2,1,0:T(8,128)(2,1)} %basis_hbm.1, f32[16,64,64]{2,1,0:T(8,128)} %leaf_move_hbm.1, ...), custom_call_target="tpu_custom_call" | custom-call | tf_op jit(solution)/shard_map/pallas_call | solution.py:432
  44.9 61.3 %shard_map.120 = (f32[7,64,64]{2,1,0:T(8,128)}, bf16[16,64,128]{2,1,0:T(8,128)(2,1)}, f32[15,64,64]{2,1,0:T(8,128)}, bf16[16,4,64,64]{3,2,1,0:T(8,128)(2,1)}, f32[4,64,64]{2,1,0:T(8,128)}) custom-call(f32[7,64,64]{2,1,0:T(8,128)} %get-tuple-element.15.gram, bf16[16,64,128]{2,1,0:T(8,128)(2,1)} %get-tuple-element.16.q, ...), custom_call_target="tpu_custom_call" | custom-call | tf_op jit(solution)/shard_map/pallas_call | solution.py:482
  (1 shorter events, 0.0 us)
Async XLA Ops:
  0.6 1.2 %copy-start = (bf16[128,64,64]{0,2,1:T(8,128)(2,1)S(1)}, bf16[128,64,64]{0,2,1:T(8,128)(2,1)}, u32[]{:S(2)}) copy-start(bf16[128,64,64]{0,2,1:T(8,128)(2,1)} %param.12) | copy-start | bytes 3145732

commit v3 on v2

--- a/solution.py
+++ b/solution.py
@@ -118,7 +118,7 @@
     basis_hbm,
     leaf_move_hbm,
     inner_move_hbm,
-    moves_hbm,
+    table_hbm,
     coupling_hbm,
     index_hbm,
     mask_hbm,
@@ -136,6 +136,7 @@
     basis,
     leaf_move,
     inner_move,
+    table,
     moves,
     coupling,
     index,
@@ -143,7 +144,9 @@
     work,
     done,
     extended,
+    packed,
     half_ref,
+    squares,
     send,
     recv,
     row_send,
@@ -174,7 +177,7 @@
             (pairing_hbm, pairing),
             (leaf_move_hbm, leaf_move),
             (inner_move_hbm, inner_move),
-            (moves_hbm, moves),
+            (table_hbm, table),
             (coupling_hbm, coupling),
             (index_hbm, index),
             (mask_hbm, mask),
@@ -251,8 +254,8 @@
         grams.extend(finish_exchange(going[-1]))
         if len(going) < len(groups):
             level = len(grams)
-            near = moves[level - 1]
-            far = split(dot_nn(near, moves[level]))
+            near = unpack(moves[level - 1]).astype(BF16)
+            far = split(dot_nn(near, unpack(moves[level]).astype(BF16)))
             terms = [carry((near, None), grams[-1]), carry(far, grams[-1])]
             going.append(start_exchange(len(going), terms))
 
@@ -282,6 +285,16 @@
     going.append(start_exchange(0, [root]))
     for j in (4, 5, 6, 7):
         loads[j].wait()
+    level = lax.broadcasted_iota(jnp.int32, (8, n_leaf), 0)
+    column = lax.broadcasted_iota(jnp.int32, (8, n_leaf), 1)
+    choose = jnp.zeros((8, n_leaf), F32)
+    for j in range(1, depth):
+        owner = me // (1 << j) * (1 << j) + (1 << (j - 1))
+        choose = jnp.where((level == j - 1) & (column == owner), 1.0, choose)
+    choose = choose.astype(BF16)
+    for b in range(size // 2):
+        both = jnp.concatenate([table[b], table[size // 2 + b]], axis=0)
+        moves[:, b, :] = dot_nt(choose, both)[: depth - 1]
 
     rows = 16
     for k in range(0, size, rows):
@@ -291,12 +304,14 @@
 
     keep = upper_mask(size)
     for i in range(leaves):
-        extended[halo + i] = jnp.where(keep, done[i, :, 0:size], 0.0).astype(BF16)
+        low = jnp.where(keep, done[i, :, 0:size], 0.0)
+        extended[halo + i] = low.astype(BF16)
+        packed[halo + i] = pack(low).astype(BF16)
     halo_copies = []
     for j, (peer, source, target) in enumerate(((after, leaves, 0), (before, halo, halo + leaves))):
         copy = pltpu.make_async_remote_copy(
-            src_ref=extended.at[pl.ds(source, halo)],
-            dst_ref=extended.at[pl.ds(target, halo)],
+            src_ref=packed.at[pl.ds(source, halo)],
+            dst_ref=packed.at[pl.ds(target, halo)],
             send_sem=halo_send_sem.at[j],
             recv_sem=halo_recv_sem.at[j],
             device_id={"leaf": peer},
@@ -307,22 +322,15 @@
     for t in range(leaves):
         for s in range(slots):
             half_ref[t, s] = dot_nn(extended[halo + t], coupling[t, s]).astype(BF16)
-    begin = pl.multiple_of(blk * part, part)
-    for i in range(leaves):
-        weights = (math.sqrt(panels) * done[i, :, size : 2 * size]).astype(BF16)
-        q_out[i] = dot_nn(weights, basis[i, :, pl.ds(begin, part)]).astype(BF16)
-    for i in range(inner):
-        inner_out[i] = jnp.where(keep, done[leaves + i, :, 0:size], 0.0)
-    store_out(q_out, q_hbm)
-    store_out(inner_out, inner_hbm)
-
     for copy in halo_copies:
         copy.wait_recv()
+    for i in range(halo):
+        extended[i] = unpack(packed[i])
+        extended[halo + leaves + i] = unpack(packed[halo + leaves + i])
     per = leaves // blocks
     base = me * leaves - halo
     row_scale = 1.0 / (slots * blocks * size)
     row_copies = []
-    own_rows = []
     for d in range(1, blocks + 1):
         peer = lax.rem(blk + d, blocks)
         for i in range(per):
@@ -335,11 +343,10 @@
                 projected[t, s] = value
                 term = dot_nt(value, value)
                 square = term if square is None else square + term
-            if d < blocks:
-                row_send[d - 1, i] = (square * row_scale).astype(BF16)
-            else:
-                own_rows.append(square * row_scale)
+            squares[d - 1, i] = square * row_scale
         if d < blocks:
+            for i in range(per):
+                row_send[d - 1, i] = pack(squares[d - 1, i]).astype(BF16)
             copy = pltpu.make_async_remote_copy(
                 src_ref=row_send.at[d - 1],
                 dst_ref=row_recv.at[d - 1],
@@ -350,6 +357,14 @@
             copy.start()
             row_copies.append(copy)
     store_out(projected, projected_hbm)
+    begin = pl.multiple_of(blk * part, part)
+    for i in range(leaves):
+        weights = (math.sqrt(panels) * done[i, :, size : 2 * size]).astype(BF16)
+        q_out[i] = dot_nn(weights, basis[i, :, pl.ds(begin, part)]).astype(BF16)
+    for i in range(inner):
+        inner_out[i] = jnp.where(keep, done[leaves + i, :, 0:size], 0.0)
+    store_out(q_out, q_hbm)
+    store_out(inner_out, inner_hbm)
     advance()
     for i in range(depth):
         gram_out[i] = grams[i]
@@ -357,10 +372,10 @@
     for copy in row_copies:
         copy.wait_recv()
     for i in range(per):
-        square = own_rows[i]
-        for d in range(blocks - 1):
+        square = row_recv[0, i].astype(F32)
+        for d in range(1, blocks - 1):
             square = square + row_recv[d, i].astype(F32)
-        weight_out[i] = square
+        weight_out[i] = squares[blocks - 1, i] + unpack(square)
     store_out(weight_out, weight_hbm)
     for started in going:
         for copy, _, _ in started:
@@ -372,22 +387,53 @@
 
 
 def last_kernel(
-    gram, q, inner, projected, weight, upper_out, q_out, inner_out, projected_out, weight_out, work, done, sem
+    gram_hbm,
+    q,
+    inner,
+    projected,
+    weight,
+    upper_out,
+    q_out,
+    inner_out,
+    projected_out,
+    weight_out,
+    gram,
+    q_held,
+    inner_held,
+    projected_held,
+    weight_held,
+    work,
+    done,
+    gram_sem,
+    in_sem,
+    out_sem,
 ):
     depth, size, _ = gram.shape
-    stores = []
-    for j, (source, target) in enumerate(
-        ((projected, projected_out), (q, q_out), (inner, inner_out), (weight, weight_out))
+    first = pltpu.make_async_copy(gram_hbm, gram, gram_sem)
+    first.start()
+    loads, stores = [], []
+    for j, (source, held, target) in enumerate(
+        (
+            (projected, projected_held, projected_out),
+            (q, q_held, q_out),
+            (inner, inner_held, inner_out),
+            (weight, weight_held, weight_out),
+        )
     ):
-        store = pltpu.make_async_copy(source, target, sem.at[j])
-        store.start()
-        stores.append(store)
+        loads.append(pltpu.make_async_copy(source, held, in_sem.at[j]))
+        stores.append(pltpu.make_async_copy(held, target, out_sem.at[j]))
+        loads[-1].start()
+    first.wait()
     for i in range(depth):
         work[i, :, 0:size] = gram[i]
         work[i, :, size : 2 * size] = jnp.zeros((size, size), F32)
     rows = 8
     for k in range(0, size, rows):
         factor_panel(work, done, 0, depth, rows, k, panel_ahead)
+        if k == 3 * rows:
+            for load, store in zip(loads, stores):
+                load.wait()
+                store.start()
     keep = upper_mask(size)
     for i in range(depth):
         upper_out[i] = jnp.where(keep, done[i, :, 0:size], 0.0)
@@ -413,14 +459,6 @@
     part = panels // blocks
     vmem = pl.BlockSpec(memory_space=VMEM)
     anywhere = pl.BlockSpec(memory_space=pl.ANY)
-
-    me = lax.axis_index("leaf")
-    level = jnp.arange(1, depth, dtype=jnp.int32)
-    owner = (me >> level << level) + (1 << (level - 1))
-    choose = (owner[:, None] == jnp.arange(n_leaf, dtype=jnp.int32)[None, :]).astype(BF16)
-    moves = jnp.einsum("rn,nba->rba", choose, upper_transfer, preferred_element_type=F32).astype(
-        BF16
-    )
 
     n_recv = 1 + 4 * ((depth - 1) // 2)
     n_send = 1 + 2 * ((depth - 1) // 2)
@@ -444,18 +482,21 @@
             VMEM((leaves, size, panels), BF16),
             VMEM((leaves, size, size), F32),
             VMEM((inner, size, size), F32),
-            VMEM((depth - 1, size, size), BF16),
+            VMEM((size, size, n_leaf), BF16),
+            VMEM((depth - 1, size // 2, 2 * size), F32),
             VMEM(coupling.shape, BF16),
             SMEM((slots, leaves), jnp.int32),
             SMEM((slots, leaves), jnp.int32),
             VMEM((leaves + inner, size, 2 * size), F32),
             VMEM((leaves + inner, size, 2 * size), F32),
             VMEM((2 * leaves, size, size), BF16),
+            VMEM((2 * leaves, size // 2, 2 * size), BF16),
             VMEM((leaves, slots, size, size), BF16),
+            VMEM((blocks, leaves // blocks, size, size), F32),
             VMEM((n_send, size // 2, 2 * size), F32),
             VMEM((n_recv, size // 2, 2 * size), F32),
-            VMEM((blocks - 1, leaves // blocks, size, size), BF16),
-            VMEM((blocks - 1, leaves // blocks, size, size), BF16),
+            VMEM((blocks - 1, leaves // blocks, size // 2, 2 * size), BF16),
+            VMEM((blocks - 1, leaves // blocks, size // 2, 2 * size), BF16),
             pltpu.SemaphoreType.DMA((8,)),
             pltpu.SemaphoreType.DMA((5,)),
             pltpu.SemaphoreType.DMA((n_recv,)),
@@ -473,7 +514,7 @@
         leaf_basis,
         leaf_transfer,
         inner_transfer[0],
-        moves,
+        jnp.transpose(upper_transfer, (1, 2, 0)),
         coupling,
         source_cluster_index.T,
         coupling_slot_mask.T,
@@ -482,11 +523,18 @@
     upper_factor, q, inner_factor, projected, row_weight = pl.pallas_call(
         last_kernel,
         out_shape=(upper_shape, q_shape, inner_shape, projected_shape, weight_shape),
-        in_specs=[vmem] + [anywhere] * 4,
+        in_specs=[anywhere] * 5,
         out_specs=(vmem,) + (anywhere,) * 4,
         scratch_shapes=[
+            VMEM(upper_shape.shape, F32),
+            VMEM(q_shape.shape, BF16),
+            VMEM(inner_shape.shape, F32),
+            VMEM(coupling.shape, BF16),
+            VMEM(weight_shape.shape, F32),
             VMEM((depth, size, 2 * size), F32),
             VMEM((depth, size, 2 * size), F32),
+            pltpu.SemaphoreType.DMA,
+            pltpu.SemaphoreType.DMA((4,)),
             pltpu.SemaphoreType.DMA((4,)),
         ],
         compiler_params=pltpu.CompilerParams(vmem_limit_bytes=60 * 2**20),

time: 108 us -> 48.7 us (0.45)
  the two profiles are of different devices: /device:TPU:6 before, /device:TPU:1 now
where the time goes in v3:
time: 48.7 us; the launch traced here: 48.6 us
  Pallas kernels  48 us (99%)
  between operations  0.64 us (1%)
    pallas_call x1, Pallas kernels, local(): pl.pallas_call(tree_kernel, out_shape=(q_shape, inner_shape, upper_shape,...  41.7 us
    pallas_call x1, Pallas kernels, local(): pl.pallas_call(last_kernel, out_shape=(upper_shape, q_shape, inner_shape,...  6.25 us

profile of v3, /device:TPU:1, one launch (start us, length us, event | category | flops | bytes accessed | tf_op | source)
XLA Modules:
  0.0 48.6 jit_solution(12679859203558985430)
XLA Ops:
  0.6 41.7 %shard_map.119 = (bf16[16,64,128]{2,1,0:T(8,128)(2,1)}, f32[15,64,64]{2,1,0:T(8,128)}, f32[7,64,64]{2,1,0:T(8,128)}, bf16[16,4,64,64]{3,2,1,0:T(8,128)(2,1)}, f32[4,64,64]{2,1,0:T(8,128)}) custom-call(s32[1,16]{1,0:T(1,128)} %pairing_hbm.1, bf16[16,64,512]{2,1,0:T(8,128)(2,1)} %basis_hbm.1, f32[16,64,64]{2,1,0:T(8,128)} %leaf_move_hbm.1, ...), custom_call_target="tpu_custom_call" | custom-call | tf_op jit(solution)/shard_map/pallas_call | solution.py:470
  42.3 6.2 %shard_map.120 = (f32[7,64,64]{2,1,0:T(8,128)}, bf16[16,64,128]{2,1,0:T(8,128)(2,1)}, f32[15,64,64]{2,1,0:T(8,128)}, bf16[16,4,64,64]{3,2,1,0:T(8,128)(2,1)}, f32[4,64,64]{2,1,0:T(8,128)}) custom-call(f32[7,64,64]{2,1,0:T(8,128)} %get-tuple-element.15.gram_hbm, bf16[16,64,128]{2,1,0:T(8,128)(2,1)} %get-tuple-element.16.q, ...), custom_call_target="tpu_custom_call" | custom-call | tf_op jit(solution)/shard_map/pallas_call | solution.py:523

commit v4 on v3

--- a/solution.py
+++ b/solution.py
@@ -299,7 +299,7 @@
     rows = 16
     for k in range(0, size, rows):
         factor_panel(work, done, 0, leaves + inner, rows, k, panel_chain)
-        if k + rows < size:
+        if k % (2 * rows) == rows:
             advance()
 
     keep = upper_mask(size)
@@ -322,6 +322,15 @@
     for t in range(leaves):
         for s in range(slots):
             half_ref[t, s] = dot_nn(extended[halo + t], coupling[t, s]).astype(BF16)
+    begin = pl.multiple_of(blk * part, part)
+    for i in range(leaves):
+        weights = (math.sqrt(panels) * done[i, :, size : 2 * size]).astype(BF16)
+        q_out[i] = dot_nn(weights, basis[i, :, pl.ds(begin, part)]).astype(BF16)
+    for i in range(inner):
+        inner_out[i] = jnp.where(keep, done[leaves + i, :, 0:size], 0.0)
+    store_out(q_out, q_hbm)
+    store_out(inner_out, inner_hbm)
+
     for copy in halo_copies:
         copy.wait_recv()
     for i in range(halo):
@@ -357,16 +366,18 @@
             copy.start()
             row_copies.append(copy)
     store_out(projected, projected_hbm)
-    begin = pl.multiple_of(blk * part, part)
-    for i in range(leaves):
-        weights = (math.sqrt(panels) * done[i, :, size : 2 * size]).astype(BF16)
-        q_out[i] = dot_nn(weights, basis[i, :, pl.ds(begin, part)]).astype(BF16)
-    for i in range(inner):
-        inner_out[i] = jnp.where(keep, done[leaves + i, :, 0:size], 0.0)
-    store_out(q_out, q_hbm)
-    store_out(inner_out, inner_hbm)
     advance()
-    for i in range(depth):
+    early = len(grams)
+    for i in range(early):
+        work[i, :, 0:size] = grams[i]
+        work[i, :, size : 2 * size] = jnp.zeros((size, size), F32)
+    rows = 8
+    for k in range(0, size, rows):
+        factor_panel(work, done, 0, early, rows, k, panel_ahead)
+    for i in range(early):
+        gram_out[i] = jnp.where(keep, done[i, :, 0:size], 0.0)
+    advance()
+    for i in range(early, depth):
         gram_out[i] = grams[i]
     store_out(gram_out, gram_hbm)
     for copy in row_copies:
@@ -424,19 +435,22 @@
         stores.append(pltpu.make_async_copy(held, target, out_sem.at[j]))
         loads[-1].start()
     first.wait()
-    for i in range(depth):
-        work[i, :, 0:size] = gram[i]
+    late = work.shape[0]
+    for i in range(depth - late):
+        upper_out[i] = gram[i]
+    for i in range(late):
+        work[i, :, 0:size] = gram[depth - late + i]
         work[i, :, size : 2 * size] = jnp.zeros((size, size), F32)
-    rows = 8
+    rows = 16
     for k in range(0, size, rows):
-        factor_panel(work, done, 0, depth, rows, k, panel_ahead)
-        if k == 3 * rows:
+        factor_panel(work, done, 0, late, rows, k, panel_ahead)
+        if k == rows:
             for load, store in zip(loads, stores):
                 load.wait()
                 store.start()
     keep = upper_mask(size)
-    for i in range(depth):
-        upper_out[i] = jnp.where(keep, done[i, :, 0:size], 0.0)
+    for i in range(late):
+        upper_out[depth - late + i] = jnp.where(keep, done[i, :, 0:size], 0.0)
     for store in stores:
         store.wait()
 
@@ -531,8 +545,8 @@
             VMEM(inner_shape.shape, F32),
             VMEM(coupling.shape, BF16),
             VMEM(weight_shape.shape, F32),
-            VMEM((depth, size, 2 * size), F32),
-            VMEM((depth, size, 2 * size), F32),
+            VMEM((2, size, 2 * size), F32),
+            VMEM((2, size, 2 * size), F32),
             pltpu.SemaphoreType.DMA,
             pltpu.SemaphoreType.DMA((4,)),
             pltpu.SemaphoreType.DMA((4,)),

time: 48.7 us -> 44.8 us (0.920)
  the two profiles are of different devices: /device:TPU:1 before, /device:TPU:6 now
where the time goes in v4:
time: 44.8 us; the launch traced here: 44.7 us
  Pallas kernels  43.9 us (98%)
  between operations  0.8 us (2%)
    pallas_call x1, Pallas kernels, local(): pl.pallas_call(tree_kernel, out_shape=(q_shape, inner_shape, upper_shape,...  39.2 us
    pallas_call x1, Pallas kernels, local(): pl.pallas_call(last_kernel, out_shape=(upper_shape, q_shape, inner_shape,...  4.69 us

profile of v4, /device:TPU:6, one launch (start us, length us, event | category | flops | bytes accessed | tf_op | source)
XLA Modules:
  0.0 44.7 jit_solution(17199566272227059000)
XLA Ops:
  0.6 39.2 %shard_map.119 = (bf16[16,64,128]{2,1,0:T(8,128)(2,1)}, f32[15,64,64]{2,1,0:T(8,128)}, f32[7,64,64]{2,1,0:T(8,128)}, bf16[16,4,64,64]{3,2,1,0:T(8,128)(2,1)}, f32[4,64,64]{2,1,0:T(8,128)}) custom-call(s32[1,16]{1,0:T(1,128)} %pairing_hbm.1, bf16[16,64,512]{2,1,0:T(8,128)(2,1)} %basis_hbm.1, f32[16,64,64]{2,1,0:T(8,128)} %leaf_move_hbm.1, ...), custom_call_target="tpu_custom_call" | custom-call | tf_op jit(solution)/shard_map/pallas_call | solution.py:484
  39.8 4.7 %shard_map.120 = (f32[7,64,64]{2,1,0:T(8,128)}, bf16[16,64,128]{2,1,0:T(8,128)(2,1)}, f32[15,64,64]{2,1,0:T(8,128)}, bf16[16,4,64,64]{3,2,1,0:T(8,128)(2,1)}, f32[4,64,64]{2,1,0:T(8,128)}) custom-call(f32[7,64,64]{2,1,0:T(8,128)} %get-tuple-element.15.gram_hbm, bf16[16,64,128]{2,1,0:T(8,128)(2,1)} %get-tuple-element.16.q, ...), custom_call_target="tpu_custom_call" | custom-call | tf_op jit(solution)/shard_map/pallas_call | solution.py:537

commit v5 on v4

--- a/solution.py
+++ b/solution.py
@@ -124,12 +124,12 @@
     mask_hbm,
     q_hbm,
     inner_hbm,
-    gram_hbm,
+    upper_hbm,
     projected_hbm,
     weight_hbm,
     q_out,
     inner_out,
-    gram_out,
+    upper_out,
     projected,
     weight_out,
     pairing,
@@ -138,6 +138,7 @@
     inner_move,
     table,
     moves,
+    path,
     coupling,
     index,
     mask,
@@ -168,7 +169,7 @@
     n_leaf, blocks = lax.axis_size("leaf"), lax.axis_size("blk")
     me, blk = lax.axis_index("leaf"), lax.axis_index("blk")
     after, before = lax.rem(me + 1, n_leaf), lax.rem(me + n_leaf - 1, n_leaf)
-    depth = gram_out.shape[0]
+    depth = upper_out.shape[0]
 
     loads = []
     for j, (source, target) in enumerate(
@@ -253,10 +254,11 @@
     def advance():
         grams.extend(finish_exchange(going[-1]))
         if len(going) < len(groups):
-            level = len(grams)
-            near = unpack(moves[level - 1]).astype(BF16)
-            far = split(dot_nn(near, unpack(moves[level]).astype(BF16)))
-            terms = [carry((near, None), grams[-1]), carry(far, grams[-1])]
+            at = 3 * (len(going) - 1)
+            terms = [
+                carry((path[at], None), grams[-1]),
+                carry((path[at + 1], path[at + 2]), grams[-1]),
+            ]
             going.append(start_exchange(len(going), terms))
 
     identity = eye(size)
@@ -295,11 +297,17 @@
     for b in range(size // 2):
         both = jnp.concatenate([table[b], table[size // 2 + b]], axis=0)
         moves[:, b, :] = dot_nt(choose, both)[: depth - 1]
+    for j in range(len(groups) - 1):
+        near = unpack(moves[2 * j]).astype(BF16)
+        path[3 * j] = near
+        far_h, far_l = split(dot_nn(near, unpack(moves[2 * j + 1]).astype(BF16)))
+        path[3 * j + 1] = far_h
+        path[3 * j + 2] = far_l
 
     rows = 16
     for k in range(0, size, rows):
         factor_panel(work, done, 0, leaves + inner, rows, k, panel_chain)
-        if k % (2 * rows) == rows:
+        if k % (2 * rows) == 0:
             advance()
 
     keep = upper_mask(size)
@@ -331,6 +339,7 @@
     store_out(q_out, q_hbm)
     store_out(inner_out, inner_hbm)
 
+    advance()
     for copy in halo_copies:
         copy.wait_recv()
     for i in range(halo):
@@ -367,19 +376,15 @@
             row_copies.append(copy)
     store_out(projected, projected_hbm)
     advance()
-    early = len(grams)
-    for i in range(early):
+    for i in range(depth):
         work[i, :, 0:size] = grams[i]
         work[i, :, size : 2 * size] = jnp.zeros((size, size), F32)
     rows = 8
     for k in range(0, size, rows):
-        factor_panel(work, done, 0, early, rows, k, panel_ahead)
-    for i in range(early):
-        gram_out[i] = jnp.where(keep, done[i, :, 0:size], 0.0)
-    advance()
-    for i in range(early, depth):
-        gram_out[i] = grams[i]
-    store_out(gram_out, gram_hbm)
+        factor_panel(work, done, 0, depth, rows, k, panel_ahead)
+    for i in range(depth):
+        upper_out[i] = jnp.where(keep, done[i, :, 0:size], 0.0)
+    store_out(upper_out, upper_hbm)
     for copy in row_copies:
         copy.wait_recv()
     for i in range(per):
@@ -397,60 +402,18 @@
         store.wait()
 
 
-def last_kernel(
-    gram_hbm,
-    q,
-    inner,
-    projected,
-    weight,
-    upper_out,
-    q_out,
-    inner_out,
-    projected_out,
-    weight_out,
-    gram,
-    q_held,
-    inner_held,
-    projected_held,
-    weight_held,
-    work,
-    done,
-    gram_sem,
-    in_sem,
-    out_sem,
-):
-    depth, size, _ = gram.shape
-    first = pltpu.make_async_copy(gram_hbm, gram, gram_sem)
-    first.start()
+def last_kernel(*refs):
+    count = (len(refs) - 2) // 3
+    in_sem, out_sem = refs[3 * count :]
     loads, stores = [], []
-    for j, (source, held, target) in enumerate(
-        (
-            (projected, projected_held, projected_out),
-            (q, q_held, q_out),
-            (inner, inner_held, inner_out),
-            (weight, weight_held, weight_out),
-        )
-    ):
-        loads.append(pltpu.make_async_copy(source, held, in_sem.at[j]))
-        stores.append(pltpu.make_async_copy(held, target, out_sem.at[j]))
+    for j in range(count):
+        held = refs[2 * count + j]
+        loads.append(pltpu.make_async_copy(refs[j], held, in_sem.at[j]))
+        stores.append(pltpu.make_async_copy(held, refs[count + j], out_sem.at[j]))
         loads[-1].start()
-    first.wait()
-    late = work.shape[0]
-    for i in range(depth - late):
-        upper_out[i] = gram[i]
-    for i in range(late):
-        work[i, :, 0:size] = gram[depth - late + i]
-        work[i, :, size : 2 * size] = jnp.zeros((size, size), F32)
-    rows = 16
-    for k in range(0, size, rows):
-        factor_panel(work, done, 0, late, rows, k, panel_ahead)
-        if k == rows:
-            for load, store in zip(loads, stores):
-                load.wait()
-                store.start()
-    keep = upper_mask(size)
-    for i in range(late):
-        upper_out[depth - late + i] = jnp.where(keep, done[i, :, 0:size], 0.0)
+    for load, store in zip(loads, stores):
+        load.wait()
+        store.start()
     for store in stores:
         store.wait()
 
@@ -471,7 +434,6 @@
     depth = n_leaf.bit_length() - 1
     slots = coupling.shape[1]
     part = panels // blocks
-    vmem = pl.BlockSpec(memory_space=VMEM)
     anywhere = pl.BlockSpec(memory_space=pl.ANY)
 
     n_recv = 1 + 4 * ((depth - 1) // 2)
@@ -481,9 +443,10 @@
     upper_shape = jax.ShapeDtypeStruct((depth, size, size), F32)
     projected_shape = jax.ShapeDtypeStruct(coupling.shape, BF16)
     weight_shape = jax.ShapeDtypeStruct((leaves // blocks, size, size), F32)
-    q, inner_factor, upper_gram, projected, row_weight = pl.pallas_call(
+    shapes = (q_shape, inner_shape, upper_shape, projected_shape, weight_shape)
+    results = pl.pallas_call(
         tree_kernel,
-        out_shape=(q_shape, inner_shape, upper_shape, projected_shape, weight_shape),
+        out_shape=shapes,
         in_specs=[anywhere] * 8,
         out_specs=(anywhere,) * 5,
         scratch_shapes=[
@@ -498,6 +461,7 @@
             VMEM((inner, size, size), F32),
             VMEM((size, size, n_leaf), BF16),
             VMEM((depth - 1, size // 2, 2 * size), F32),
+            VMEM((3 * ((depth - 1) // 2), size, size), BF16),
             VMEM(coupling.shape, BF16),
             SMEM((slots, leaves), jnp.int32),
             SMEM((slots, leaves), jnp.int32),
@@ -534,25 +498,15 @@
         coupling_slot_mask.T,
     )
 
-    upper_factor, q, inner_factor, projected, row_weight = pl.pallas_call(
+    q, inner_factor, upper_factor, projected, row_weight = pl.pallas_call(
         last_kernel,
-        out_shape=(upper_shape, q_shape, inner_shape, projected_shape, weight_shape),
+        out_shape=shapes,
         in_specs=[anywhere] * 5,
-        out_specs=(vmem,) + (anywhere,) * 4,
-        scratch_shapes=[
-            VMEM(upper_shape.shape, F32),
-            VMEM(q_shape.shape, BF16),
-            VMEM(inner_shape.shape, F32),
-            VMEM(coupling.shape, BF16),
-            VMEM(weight_shape.shape, F32),
-            VMEM((2, size, 2 * size), F32),
-            VMEM((2, size, 2 * size), F32),
-            pltpu.SemaphoreType.DMA,
-            pltpu.SemaphoreType.DMA((4,)),
-            pltpu.SemaphoreType.DMA((4,)),
-        ],
+        out_specs=(anywhere,) * 5,
+        scratch_shapes=[VMEM(shape.shape, shape.dtype) for shape in shapes]
+        + [pltpu.SemaphoreType.DMA((5,)), pltpu.SemaphoreType.DMA((5,))],
         compiler_params=pltpu.CompilerParams(vmem_limit_bytes=60 * 2**20),
-    )(upper_gram, q, inner_factor, projected, row_weight)
+    )(*results)
     return (q, inner_factor[None], upper_factor[None], projected, row_weight)
 
 

time: 44.8 us -> 45 us (level)
  no operation moved by 1% of the time
where the time goes in v5:
time: 45 us; the launch traced here: 44.9 us
  Pallas kernels  44.2 us (98%)
  between operations  0.64 us (1%)
    pallas_call x1, Pallas kernels, local(): pl.pallas_call(tree_kernel, out_shape=shapes, in_specs=[anywhere] * 8, ou...  41.6 us
    pallas_call x1, Pallas kernels, local(): pl.pallas_call(last_kernel, out_shape=shapes, in_specs=[anywhere] * 5, ou...  2.62 us

profile of v5, /device:TPU:6, one launch (start us, length us, event | category | flops | bytes accessed | tf_op | source)
XLA Modules:
  0.0 44.9 jit_solution(13357657697333702060)
XLA Ops:
  0.6 41.6 %shard_map.119 = (bf16[16,64,128]{2,1,0:T(8,128)(2,1)}, f32[15,64,64]{2,1,0:T(8,128)}, f32[7,64,64]{2,1,0:T(8,128)}, bf16[16,4,64,64]{3,2,1,0:T(8,128)(2,1)}, f32[4,64,64]{2,1,0:T(8,128)}) custom-call(s32[1,16]{1,0:T(1,128)} %pairing_hbm.1, bf16[16,64,512]{2,1,0:T(8,128)(2,1)} %basis_hbm.1, f32[16,64,64]{2,1,0:T(8,128)} %leaf_move_hbm.1, ...), custom_call_target="tpu_custom_call" | custom-call | tf_op jit(solution)/shard_map/pallas_call | solution.py:447
  42.2 2.6 %shard_map.120 = (bf16[16,64,128]{2,1,0:T(8,128)(2,1)}, f32[15,64,64]{2,1,0:T(8,128)}, f32[7,64,64]{2,1,0:T(8,128)}, bf16[16,4,64,64]{3,2,1,0:T(8,128)(2,1)}, f32[4,64,64]{2,1,0:T(8,128)}) custom-call(bf16[16,64,128]{2,1,0:T(8,128)(2,1)} %get-tuple-element.15.refs_0_, f32[15,64,64]{2,1,0:T(8,128)} %get-tuple-element.16.refs_1_, ...), custom_call_target="tpu_custom_call" | custom-call | tf_op jit(solution)/shard_map/pallas_call | solution.py:501

commit v6 on v5

--- a/solution.py
+++ b/solution.py
@@ -12,6 +12,7 @@
 BF16 = jnp.bfloat16
 VMEM = pltpu.VMEM
 SMEM = pltpu.SMEM
+PARTNERS = ((1,), (2, 4, 6), (8,), (24,), (32, 64, 96))
 
 
 def split(x):
@@ -203,7 +204,7 @@
             bit *= 2
         return out
 
-    groups = [(1,)] + [(2 << (2 * g), 4 << (2 * g), 6 << (2 * g)) for g in range((depth - 1) // 2)]
+    groups = PARTNERS
     barrier = pltpu.get_barrier_semaphore()
     total = 0
     for group in groups:
@@ -249,16 +250,15 @@
             sums[source] = sums.get(source, send[source]) + recv[at]
         return [unpack(sums[s]) for s in sorted(sums)]
 
-    grams, going = [], []
+    grams, going, paths = [], [], {}
 
     def advance():
         grams.extend(finish_exchange(going[-1]))
         if len(going) < len(groups):
-            at = 3 * (len(going) - 1)
-            terms = [
-                carry((path[at], None), grams[-1]),
-                carry((path[at + 1], path[at + 2]), grams[-1]),
-            ]
+            at = paths[len(going)]
+            terms = [carry((path[at], None), grams[-1])]
+            if len(groups[len(going)]) > 1:
+                terms.append(carry((path[at + 1], path[at + 2]), grams[-1]))
             going.append(start_exchange(len(going), terms))
 
     identity = eye(size)
@@ -297,12 +297,17 @@
     for b in range(size // 2):
         both = jnp.concatenate([table[b], table[size // 2 + b]], axis=0)
         moves[:, b, :] = dot_nt(choose, both)[: depth - 1]
-    for j in range(len(groups) - 1):
-        near = unpack(moves[2 * j]).astype(BF16)
-        path[3 * j] = near
-        far_h, far_l = split(dot_nn(near, unpack(moves[2 * j + 1]).astype(BF16)))
-        path[3 * j + 1] = far_h
-        path[3 * j + 2] = far_l
+    at, j = 0, 0
+    for step in range(1, len(groups)):
+        paths[step] = at
+        near = unpack(moves[j]).astype(BF16)
+        path[at] = near
+        at, j = at + 1, j + 1
+        if len(groups[step]) > 1:
+            far_h, far_l = split(dot_nn(near, unpack(moves[j]).astype(BF16)))
+            path[at] = far_h
+            path[at + 1] = far_l
+            at, j = at + 2, j + 1
 
     rows = 16
     for k in range(0, size, rows):
@@ -327,6 +332,7 @@
         copy.start()
         halo_copies.append(copy)
 
+    advance()
     for t in range(leaves):
         for s in range(slots):
             half_ref[t, s] = dot_nn(extended[halo + t], coupling[t, s]).astype(BF16)
@@ -436,8 +442,9 @@
     part = panels // blocks
     anywhere = pl.BlockSpec(memory_space=pl.ANY)
 
-    n_recv = 1 + 4 * ((depth - 1) // 2)
-    n_send = 1 + 2 * ((depth - 1) // 2)
+    n_recv = sum(1 if len(group) == 1 else 4 for group in PARTNERS)
+    n_send = sum(1 if len(group) == 1 else 2 for group in PARTNERS)
+    n_path = sum(1 if len(group) == 1 else 3 for group in PARTNERS[1:])
     q_shape = jax.ShapeDtypeStruct((leaves, size, part), BF16)
     inner_shape = jax.ShapeDtypeStruct((inner, size, size), F32)
     upper_shape = jax.ShapeDtypeStruct((depth, size, size), F32)
@@ -461,7 +468,7 @@
             VMEM((inner, size, size), F32),
             VMEM((size, size, n_leaf), BF16),
             VMEM((depth - 1, size // 2, 2 * size), F32),
-            VMEM((3 * ((depth - 1) // 2), size, size), BF16),
+            VMEM((n_path, size, size), BF16),
             VMEM(coupling.shape, BF16),
             SMEM((slots, leaves), jnp.int32),
             SMEM((slots, leaves), jnp.int32),

time: 45 us -> 46.1 us (1.024)
  Pallas kernels: 44.2 us -> 45.3 us
    pallas_call x1, Pallas kernels: 41.6 us -> 42.7 us  [local(): pl.pallas_call(tree_kernel, out_shape=shapes, in_specs=[anywhere] * 8, ou...]
where the time goes in v6:
time: 46.1 us; the launch traced here: 45.9 us
  Pallas kernels  45.3 us (98%)
  between operations  0.64 us (1%)
    pallas_call x1, Pallas kernels, local(): pl.pallas_call(tree_kernel, out_shape=shapes, in_specs=[anywhere] * 8, ou...  42.7 us
    pallas_call x1, Pallas kernels, local(): pl.pallas_call(last_kernel, out_shape=shapes, in_specs=[anywhere] * 5, ou...  2.62 us

profile of v6, /device:TPU:6, one launch (start us, length us, event | category | flops | bytes accessed | tf_op | source)
XLA Modules:
  0.0 45.9 jit_solution(6998507566559589042)
XLA Ops:
  0.6 42.7 %shard_map.119 = (bf16[16,64,128]{2,1,0:T(8,128)(2,1)}, f32[15,64,64]{2,1,0:T(8,128)}, f32[7,64,64]{2,1,0:T(8,128)}, bf16[16,4,64,64]{3,2,1,0:T(8,128)(2,1)}, f32[4,64,64]{2,1,0:T(8,128)}) custom-call(s32[1,16]{1,0:T(1,128)} %pairing_hbm.1, bf16[16,64,512]{2,1,0:T(8,128)(2,1)} %basis_hbm.1, f32[16,64,64]{2,1,0:T(8,128)} %leaf_move_hbm.1, ...), custom_call_target="tpu_custom_call" | custom-call | tf_op jit(solution)/shard_map/pallas_call | solution.py:454
  43.3 2.6 %shard_map.120 = (bf16[16,64,128]{2,1,0:T(8,128)(2,1)}, f32[15,64,64]{2,1,0:T(8,128)}, f32[7,64,64]{2,1,0:T(8,128)}, bf16[16,4,64,64]{3,2,1,0:T(8,128)(2,1)}, f32[4,64,64]{2,1,0:T(8,128)}) custom-call(bf16[16,64,128]{2,1,0:T(8,128)(2,1)} %get-tuple-element.15.refs_0_, f32[15,64,64]{2,1,0:T(8,128)} %get-tuple-element.16.refs_1_, ...), custom_call_target="tpu_custom_call" | custom-call | tf_op jit(solution)/shard_map/pallas_call | solution.py:508

commit v7 on v5

--- a/solution.py
+++ b/solution.py
@@ -12,6 +12,7 @@
 BF16 = jnp.bfloat16
 VMEM = pltpu.VMEM
 SMEM = pltpu.SMEM
+SPLIT = (1, 2)
 
 
 def split(x):
@@ -150,6 +151,7 @@
     squares,
     send,
     recv,
+    gathered,
     row_send,
     row_recv,
     in_sem,
@@ -160,6 +162,8 @@
     halo_recv_sem,
     row_send_sem,
     row_recv_sem,
+    gather_send_sem,
+    gather_recv_sem,
 ):
     leaves, size, panels = basis.shape
     inner = inner_move.shape[0]
@@ -217,6 +221,8 @@
         pl.semaphore_signal(barrier, 1, device_id={"blk": lax.rem(blk + d, blocks)})
         total += 1
 
+    share = size // 2 // blocks
+    quarter = pl.ds(pl.multiple_of(blk * share, share), share)
     used = [0, 0]
 
     def start_exchange(step, terms):
@@ -231,9 +237,10 @@
             for source in parts:
                 at = used[1]
                 used[1] += 1
+                rows = quarter if step in SPLIT else pl.ds(0, size // 2)
                 copy = pltpu.make_async_remote_copy(
-                    src_ref=send.at[source],
-                    dst_ref=recv.at[at],
+                    src_ref=send.at[source, rows],
+                    dst_ref=recv.at[at, rows],
                     send_sem=send_sem.at[at],
                     recv_sem=recv_sem.at[at],
                     device_id={"leaf": flipped(apart)},
@@ -242,6 +249,36 @@
                 started.append((copy, source, at))
         return started
 
+    gathers = []
+
+    def start_gather(started):
+        sums = {}
+        for copy, source, at in started:
+            copy.wait_recv()
+            sums[source] = sums.get(source, send[source, quarter, :]) + recv[at, quarter, :]
+        first = 2 * len(gathers)
+        copies = []
+        for j, source in enumerate(sorted(sums)):
+            gathered[first + j, quarter, :] = sums[source]
+            for d in range(1, blocks):
+                at = (first + j) * (blocks - 1) + d - 1
+                copy = pltpu.make_async_remote_copy(
+                    src_ref=gathered.at[first + j, quarter],
+                    dst_ref=gathered.at[first + j, quarter],
+                    send_sem=gather_send_sem.at[at],
+                    recv_sem=gather_recv_sem.at[at],
+                    device_id={"blk": lax.rem(blk + d, blocks)},
+                )
+                copy.start()
+                copies.append(copy)
+        gathers.append((copies, len(sums)))
+
+    def finish_gather():
+        copies, count = gathers[-1]
+        for copy in copies:
+            copy.wait_recv()
+        return [unpack(gathered[2 * (len(gathers) - 1) + j]) for j in range(count)]
+
     def finish_exchange(started):
         sums = {}
         for copy, source, at in started:
@@ -252,7 +289,10 @@
     grams, going = [], []
 
     def advance():
-        grams.extend(finish_exchange(going[-1]))
+        if len(going) - 1 in SPLIT:
+            grams.extend(finish_gather())
+        else:
+            grams.extend(finish_exchange(going[-1]))
         if len(going) < len(groups):
             at = 3 * (len(going) - 1)
             terms = [
@@ -307,8 +347,10 @@
     rows = 16
     for k in range(0, size, rows):
         factor_panel(work, done, 0, leaves + inner, rows, k, panel_chain)
-        if k % (2 * rows) == 0:
+        if k in (0, 2 * rows):
             advance()
+        if k == rows:
+            start_gather(going[-1])
 
     keep = upper_mask(size)
     for i in range(leaves):
@@ -327,6 +369,7 @@
         copy.start()
         halo_copies.append(copy)
 
+    start_gather(going[-1])
     for t in range(leaves):
         for s in range(slots):
             half_ref[t, s] = dot_nn(extended[halo + t], coupling[t, s]).astype(BF16)
@@ -396,7 +439,7 @@
     for started in going:
         for copy, _, _ in started:
             copy.wait_send()
-    for copy in halo_copies + row_copies:
+    for copy in halo_copies + row_copies + [c for copies, _ in gathers for c in copies]:
         copy.wait_send()
     for store in stores:
         store.wait()
@@ -473,6 +516,7 @@
             VMEM((blocks, leaves // blocks, size, size), F32),
             VMEM((n_send, size // 2, 2 * size), F32),
             VMEM((n_recv, size // 2, 2 * size), F32),
+            VMEM((2 * len(SPLIT), size // 2, 2 * size), F32),
             VMEM((blocks - 1, leaves // blocks, size // 2, 2 * size), BF16),
             VMEM((blocks - 1, leaves // blocks, size // 2, 2 * size), BF16),
             pltpu.SemaphoreType.DMA((8,)),
@@ -483,6 +527,8 @@
             pltpu.SemaphoreType.DMA((2,)),
             pltpu.SemaphoreType.DMA((blocks - 1,)),
             pltpu.SemaphoreType.DMA((blocks - 1,)),
+            pltpu.SemaphoreType.DMA((2 * len(SPLIT) * (blocks - 1),)),
+            pltpu.SemaphoreType.DMA((2 * len(SPLIT) * (blocks - 1),)),
         ],
         compiler_params=pltpu.CompilerParams(
             collective_id=0, has_side_effects=True, vmem_limit_bytes=60 * 2**20

time: 45 us -> 49.9 us (1.11)
  Pallas kernels: 44.2 us -> 49.1 us
    pallas_call x1, Pallas kernels: 41.6 us -> 46.4 us  [local(): pl.pallas_call(tree_kernel, out_shape=shapes, in_specs=[anywhere] * 8, ou...]
where the time goes in v7:
time: 49.9 us; the launch traced here: 49.7 us
  Pallas kernels  49.1 us (98%)
  between operations  0.64 us (1%)
    pallas_call x1, Pallas kernels, local(): pl.pallas_call(tree_kernel, out_shape=shapes, in_specs=[anywhere] * 8, ou...  46.4 us
    pallas_call x1, Pallas kernels, local(): pl.pallas_call(last_kernel, out_shape=shapes, in_specs=[anywhere] * 5, ou...  2.62 us

profile of v7, /device:TPU:6, one launch (start us, length us, event | category | flops | bytes accessed | tf_op | source)
XLA Modules:
  0.0 49.7 jit_solution(5344649051102385331)
XLA Ops:
  0.6 46.4 %shard_map.119 = (bf16[16,64,128]{2,1,0:T(8,128)(2,1)}, f32[15,64,64]{2,1,0:T(8,128)}, f32[7,64,64]{2,1,0:T(8,128)}, bf16[16,4,64,64]{3,2,1,0:T(8,128)(2,1)}, f32[4,64,64]{2,1,0:T(8,128)}) custom-call(s32[1,16]{1,0:T(1,128)} %pairing_hbm.1, bf16[16,64,512]{2,1,0:T(8,128)(2,1)} %basis_hbm.1, f32[16,64,64]{2,1,0:T(8,128)} %leaf_move_hbm.1, ...), custom_call_target="tpu_custom_call" | custom-call | tf_op jit(solution)/shard_map/pallas_call | solution.py:490
  47.1 2.6 %shard_map.120 = (bf16[16,64,128]{2,1,0:T(8,128)(2,1)}, f32[15,64,64]{2,1,0:T(8,128)}, f32[7,64,64]{2,1,0:T(8,128)}, bf16[16,4,64,64]{3,2,1,0:T(8,128)(2,1)}, f32[4,64,64]{2,1,0:T(8,128)}) custom-call(bf16[16,64,128]{2,1,0:T(8,128)(2,1)} %get-tuple-element.15.refs_0_, f32[15,64,64]{2,1,0:T(8,128)} %get-tuple-element.16.refs_1_, ...), custom_call_target="tpu_custom_call" | custom-call | tf_op jit(solution)/shard_map/pallas_call | solution.py:547

commit v8 on v4

--- a/solution.py
+++ b/solution.py
@@ -138,6 +138,7 @@
     inner_move,
     table,
     moves,
+    path,
     coupling,
     index,
     mask,
@@ -253,10 +254,11 @@
     def advance():
         grams.extend(finish_exchange(going[-1]))
         if len(going) < len(groups):
-            level = len(grams)
-            near = unpack(moves[level - 1]).astype(BF16)
-            far = split(dot_nn(near, unpack(moves[level]).astype(BF16)))
-            terms = [carry((near, None), grams[-1]), carry(far, grams[-1])]
+            at = 3 * (len(going) - 1)
+            terms = [
+                carry((path[at], None), grams[-1]),
+                carry((path[at + 1], path[at + 2]), grams[-1]),
+            ]
             going.append(start_exchange(len(going), terms))
 
     identity = eye(size)
@@ -295,11 +297,17 @@
     for b in range(size // 2):
         both = jnp.concatenate([table[b], table[size // 2 + b]], axis=0)
         moves[:, b, :] = dot_nt(choose, both)[: depth - 1]
+    for j in range(len(groups) - 1):
+        near = unpack(moves[2 * j]).astype(BF16)
+        path[3 * j] = near
+        far_h, far_l = split(dot_nn(near, unpack(moves[2 * j + 1]).astype(BF16)))
+        path[3 * j + 1] = far_h
+        path[3 * j + 2] = far_l
 
     rows = 16
     for k in range(0, size, rows):
         factor_panel(work, done, 0, leaves + inner, rows, k, panel_chain)
-        if k % (2 * rows) == rows:
+        if k % (2 * rows) == 0:
             advance()
 
     keep = upper_mask(size)
@@ -331,6 +339,7 @@
     store_out(q_out, q_hbm)
     store_out(inner_out, inner_hbm)
 
+    advance()
     for copy in halo_copies:
         copy.wait_recv()
     for i in range(halo):
@@ -366,7 +375,6 @@
             copy.start()
             row_copies.append(copy)
     store_out(projected, projected_hbm)
-    advance()
     early = len(grams)
     for i in range(early):
         work[i, :, 0:size] = grams[i]
@@ -498,6 +506,7 @@
             VMEM((inner, size, size), F32),
             VMEM((size, size, n_leaf), BF16),
             VMEM((depth - 1, size // 2, 2 * size), F32),
+            VMEM((3 * ((depth - 1) // 2), size, size), BF16),
             VMEM(coupling.shape, BF16),
             SMEM((slots, leaves), jnp.int32),
             SMEM((slots, leaves), jnp.int32),

time: 44.8 us -> 44.1 us (0.984)
  Pallas kernels: 43.9 us -> 43 us
    pallas_call x1, Pallas kernels: 39.2 us -> 38.3 us  [local(): pl.pallas_call(tree_kernel, out_shape=(q_shape, inner_shape, upper_shape,...]
where the time goes in v8:
time: 44.1 us; the launch traced here: 43.8 us
  Pallas kernels  43 us (98%)
  between operations  0.8 us (2%)
    pallas_call x1, Pallas kernels, local(): pl.pallas_call(tree_kernel, out_shape=(q_shape, inner_shape, upper_shape,...  38.3 us
    pallas_call x1, Pallas kernels, local(): pl.pallas_call(last_kernel, out_shape=(upper_shape, q_shape, inner_shape,...  4.69 us

profile of v8, /device:TPU:6, one launch (start us, length us, event | category | flops | bytes accessed | tf_op | source)
XLA Modules:
  0.0 43.8 jit_solution(2790397017996780330)
XLA Ops:
  0.6 38.3 %shard_map.119 = (bf16[16,64,128]{2,1,0:T(8,128)(2,1)}, f32[15,64,64]{2,1,0:T(8,128)}, f32[7,64,64]{2,1,0:T(8,128)}, bf16[16,4,64,64]{3,2,1,0:T(8,128)(2,1)}, f32[4,64,64]{2,1,0:T(8,128)}) custom-call(s32[1,16]{1,0:T(1,128)} %pairing_hbm.1, bf16[16,64,512]{2,1,0:T(8,128)(2,1)} %basis_hbm.1, f32[16,64,64]{2,1,0:T(8,128)} %leaf_move_hbm.1, ...), custom_call_target="tpu_custom_call" | custom-call | tf_op jit(solution)/shard_map/pallas_call | solution.py:492
  38.9 4.7 %shard_map.120 = (f32[7,64,64]{2,1,0:T(8,128)}, bf16[16,64,128]{2,1,0:T(8,128)(2,1)}, f32[15,64,64]{2,1,0:T(8,128)}, bf16[16,4,64,64]{3,2,1,0:T(8,128)(2,1)}, f32[4,64,64]{2,1,0:T(8,128)}) custom-call(f32[7,64,64]{2,1,0:T(8,128)} %get-tuple-element.15.gram_hbm, bf16[16,64,128]{2,1,0:T(8,128)(2,1)} %get-tuple-element.16.q, ...), custom_call_target="tpu_custom_call" | custom-call | tf_op jit(solution)/shard_map/pallas_call | solution.py:546

commit v9 on v8

--- a/solution.py
+++ b/solution.py
@@ -307,7 +307,7 @@
     rows = 16
     for k in range(0, size, rows):
         factor_panel(work, done, 0, leaves + inner, rows, k, panel_chain)
-        if k % (2 * rows) == 0:
+        if k < 2 * rows:
             advance()
 
     keep = upper_mask(size)

time: 44.1 us -> 43.6 us (0.989)
  Pallas kernels: 43 us -> 42.4 us
    pallas_call x1, Pallas kernels: 38.3 us -> 37.7 us  [local(): pl.pallas_call(tree_kernel, out_shape=(q_shape, inner_shape, upper_shape,...]
where the time goes in v9:
time: 43.6 us; the launch traced here: 43.2 us
  Pallas kernels  42.4 us (97%)
  between operations  0.8 us (2%)
    pallas_call x1, Pallas kernels, local(): pl.pallas_call(tree_kernel, out_shape=(q_shape, inner_shape, upper_shape,...  37.7 us
    pallas_call x1, Pallas kernels, local(): pl.pallas_call(last_kernel, out_shape=(upper_shape, q_shape, inner_shape,...  4.69 us

profile of v9, /device:TPU:6, one launch (start us, length us, event | category | flops | bytes accessed | tf_op | source)
XLA Modules:
  0.0 43.2 jit_solution(2302055323965997693)
XLA Ops:
  0.6 37.7 %shard_map.119 = (bf16[16,64,128]{2,1,0:T(8,128)(2,1)}, f32[15,64,64]{2,1,0:T(8,128)}, f32[7,64,64]{2,1,0:T(8,128)}, bf16[16,4,64,64]{3,2,1,0:T(8,128)(2,1)}, f32[4,64,64]{2,1,0:T(8,128)}) custom-call(s32[1,16]{1,0:T(1,128)} %pairing_hbm.1, bf16[16,64,512]{2,1,0:T(8,128)(2,1)} %basis_hbm.1, f32[16,64,64]{2,1,0:T(8,128)} %leaf_move_hbm.1, ...), custom_call_target="tpu_custom_call" | custom-call | tf_op jit(solution)/shard_map/pallas_call | solution.py:492
  38.4 4.7 %shard_map.120 = (f32[7,64,64]{2,1,0:T(8,128)}, bf16[16,64,128]{2,1,0:T(8,128)(2,1)}, f32[15,64,64]{2,1,0:T(8,128)}, bf16[16,4,64,64]{3,2,1,0:T(8,128)(2,1)}, f32[4,64,64]{2,1,0:T(8,128)}) custom-call(f32[7,64,64]{2,1,0:T(8,128)} %get-tuple-element.15.gram_hbm, bf16[16,64,128]{2,1,0:T(8,128)(2,1)} %get-tuple-element.16.q, ...), custom_call_target="tpu_custom_call" | custom-call | tf_op jit(solution)/shard_map/pallas_call | solution.py:546
